TPU v7x, 256 devices: a whole 4x4x8 slice. The times are simulated.
256 devices in a mesh: clusters: 64 (over z, x, core), tiles: 4 (over y).
Axes of the slice: x: 4, y: 4, z: 8, core: 2. Of those that a mesh axis runs over, the one named last changes fastest.
Arguments:
- source_points: bfloat16 [512, 30, 1024], P('clusters', None, 'tiles'), may hold values from -1.5 to 1.5
- target_points: bfloat16 [512, 30, 1024], P('clusters'), may hold values from -1.5 to 1.5
- source_potential: float32 [512, 1024], P('clusters', 'tiles'), may hold values from -66 to 66
- target_potential: float32 [512, 1024], P('clusters'), may hold values from -66 to 66
- kept_targets: int32 [512, 12], replicated, may hold values from 0 to 511, as said below
- kept_counts: int32 [512], replicated, may hold values from 1 to 12, as said below
- target_home: int32 [512], replicated, may hold values from 0 to 511, as said below
Outputs:
- source_next: float32 [512, 1024], P('clusters', 'tiles')
- target_next: float32 [512, 1024], P('clusters')
Inputs may be any that keep to these rules, and one draw needn't show every extreme that they name: `kept_counts`: every source cluster has one or more live slots; on every index of clusters one of its 8 source clusters has all 12. `kept_targets`: the 12 slots of a source cluster name distinct clusters. Call the slots of the 8 source clusters of one index of clusters one requester, and target_home[id] // 8 the owner of the cluster a slot names: the slots of one requester name at most 2 clusters of any one owner, live or not; in every draw one owner is named by 2 live slots of every requester. `target_home`: A permutation of the target cluster ids.
All inputs are finite; a program needn't handle non-finite values.
Results may differ from a plain program's by a relative error of at most 0.002.
Values may be sent and summed in bfloat16 or wider, within the bound.
A program may use at most 64 MiB of HBM per device.

v0:
```python
import jax
import jax.numpy as jnp
from jax import lax
from jax.sharding import PartitionSpec as P

epsilon_reg = 0.25
sentinel = -1e30


def combined_all(array, axis, combine):
    everything = jax.tree.map(lambda part: lax.all_gather(part, axis), array)
    leading = jax.tree.map(lambda part: part[0], everything)

    def lap(k, so_far):
        return combine(so_far, jax.tree.map(lambda part: part[k], everything))

    return lax.fori_loop(1, lax.axis_size(axis), lap, leading)


def lse_pair(first, second):
    summit = jnp.maximum(first[0], second[0])
    return (summit, first[1] * jnp.exp(first[0] - summit) + second[1] * jnp.exp(second[0] - summit))


def requester_slots(kept_targets, kept_counts, target_home, group_index, per_group):
    slot_width = kept_targets.shape[1]
    kept_rows = lax.dynamic_slice_in_dim(kept_targets, group_index * per_group, per_group, 0)
    numbers = lax.dynamic_slice_in_dim(kept_counts, group_index * per_group, per_group, 0)
    living = jnp.arange(slot_width, dtype=jnp.int32)[None, :] < numbers[:, None]
    return (jnp.take(target_home, kept_rows.reshape(-1)), living.reshape(-1))


def owner_rank(owners, living):
    serial = jnp.arange(owners.shape[0], dtype=jnp.int32)
    earlier = (
        (owners[:, None] == owners[None, :]) & living[None, :] & (serial[None, :] < serial[:, None])
    )
    return jnp.sum(earlier.astype(jnp.int32), axis=1)


def tile_stats(points, point_norms, potential, target, target_norms, target_pot):
    row_width = points.shape[1]
    block_rows = min(512, row_width)
    inner_prod = lax.dot_general(
        points, target, (((0,), (0,)), ((), ())), preferred_element_type=jnp.float32
    )
    tile_cost = 0.5 * point_norms[0:block_rows, None] + 0.5 * target_norms[None, :] - inner_prod
    row_scores = (target_pot[None, :] - tile_cost) / epsilon_reg
    row_top = jnp.max(row_scores, axis=1)
    row_tops = [row_top]
    row_sums = [jnp.sum(jnp.exp(row_scores - row_top[:, None]), axis=1)]
    col_scores = (potential[0:block_rows, None] - tile_cost) / epsilon_reg
    block_top = jnp.max(col_scores, axis=0)
    block_sum = jnp.sum(jnp.exp(col_scores - block_top[None, :]), axis=0)
    return (jnp.concatenate(row_tops), jnp.concatenate(row_sums), block_top, block_sum)


def local(
    source_points,
    target_points,
    source_potential,
    target_potential,
    kept_targets,
    kept_counts,
    target_home,
):
    group_count = lax.axis_size("clusters")
    my_group = lax.axis_index("clusters")
    per_group = source_points.shape[0]
    per_owner = target_points.shape[0]
    coords = source_points.shape[1]
    slot_width = kept_targets.shape[1]
    slot_count = per_group * slot_width
    capacity = max(2, (slot_count + group_count - 1) // group_count)
    all_points, all_potential = (source_points, source_potential)
    own_targets, target_start = (target_points, target_potential)
    row_width = all_points.shape[2]
    cluster_width = own_targets.shape[2]
    stored, living = requester_slots(kept_targets, kept_counts, target_home, my_group, per_group)
    owners = stored // per_owner
    ranks_here = owner_rank(owners, living)
    arrival = jnp.where(living, owners * capacity + ranks_here, 0)
    every_stored, every_living = jax.vmap(
        lambda group_index: requester_slots(
            kept_targets, kept_counts, target_home, group_index, per_group
        )
    )(jnp.arange(group_count, dtype=jnp.int32))
    every_owner = every_stored // per_owner
    every_rank = jax.vmap(owner_rank)(every_owner, every_living)
    owned_here = every_living & (every_owner == my_group)
    places = jnp.arange(capacity, dtype=jnp.int32)
    matched = owned_here[:, :, None] & (every_rank[:, :, None] == places[None, None, :])
    send_local = (
        jnp.sum(jnp.where(matched, (every_stored % per_owner)[:, :, None] + 1, 0), axis=1) - 1
    )
    send_valid = send_local >= 0
    send_index = jnp.maximum(send_local, 0).reshape(-1)
    source_norms = jnp.sum(jnp.square(all_points.astype(jnp.float32)), axis=1)
    picked = jnp.take(own_targets, send_index, axis=0).reshape(
        group_count, capacity, coords, cluster_width
    )
    packed = jnp.where(send_valid[:, :, None, None], picked, jnp.zeros((), jnp.bfloat16))
    arrived = lax.all_to_all(packed, "clusters", split_axis=0, concat_axis=0, tiled=True)
    slot_points = jnp.take(
        arrived.reshape(group_count * capacity, coords, cluster_width), arrival, axis=0
    )
    slot_norms = jnp.sum(jnp.square(slot_points.astype(jnp.float32)), axis=1)
    visit_order = jnp.arange(slot_count, dtype=jnp.int32)
    source_now = all_potential
    sent_pot = jnp.where(
        send_valid[:, :, None],
        jnp.take(target_start, send_index, axis=0).reshape(group_count, capacity, cluster_width),
        0.0,
    )
    got_pot = lax.all_to_all(sent_pot, "clusters", split_axis=0, concat_axis=0, tiled=True)
    slot_pot = jnp.take(got_pot.reshape(group_count * capacity, cluster_width), arrival, axis=0)

    def visit(turn, carry, slot_pot=slot_pot, source_now=source_now):
        row_peak, row_mass, col_peak, col_mass = carry
        slot_at = visit_order[turn]
        home_cluster = slot_at // slot_width
        active = living[slot_at]
        tile_row_top, tile_row_sum, tile_col_top, tile_col_sum = tile_stats(
            lax.dynamic_index_in_dim(all_points, home_cluster, 0, keepdims=False),
            lax.dynamic_index_in_dim(source_norms, home_cluster, 0, keepdims=False),
            lax.dynamic_index_in_dim(source_now, home_cluster, 0, keepdims=False),
            lax.dynamic_index_in_dim(slot_points, slot_at, 0, keepdims=False),
            lax.dynamic_index_in_dim(slot_norms, slot_at, 0, keepdims=False),
            lax.dynamic_index_in_dim(slot_pot, slot_at, 0, keepdims=False),
        )
        tile_row_top = jnp.where(active, tile_row_top, sentinel)
        tile_row_sum = jnp.where(active, tile_row_sum, 0.0)
        before = (
            lax.dynamic_index_in_dim(row_peak, home_cluster, 0, keepdims=False),
            lax.dynamic_index_in_dim(row_mass, home_cluster, 0, keepdims=False),
        )
        new_peak, new_mass = lse_pair(before, (tile_row_top, tile_row_sum))
        row_peak = lax.dynamic_update_index_in_dim(row_peak, new_peak, home_cluster, 0)
        row_mass = lax.dynamic_update_index_in_dim(row_mass, new_mass, home_cluster, 0)
        col_peak = lax.dynamic_update_index_in_dim(
            col_peak, jnp.where(active, tile_col_top, sentinel), slot_at, 0
        )
        col_mass = lax.dynamic_update_index_in_dim(
            col_mass, jnp.where(active, tile_col_sum, 0.0), slot_at, 0
        )
        return (row_peak, row_mass, col_peak, col_mass)

    start = (
        jnp.full((per_group, row_width), sentinel, jnp.float32),
        jnp.zeros((per_group, row_width), jnp.float32),
        jnp.full((slot_count, cluster_width), sentinel, jnp.float32),
        jnp.zeros((slot_count, cluster_width), jnp.float32),
    )
    row_peak, row_mass, col_peak, col_mass = lax.fori_loop(0, slot_count, visit, start)
    source_next = -epsilon_reg * (row_peak + jnp.log(row_mass))
    back_group = jnp.where(living, owners, group_count)
    back_peak = (
        jnp.full((group_count, capacity, cluster_width), sentinel, jnp.float32)
        .at[back_group, ranks_here]
        .set(col_peak, mode="drop")
    )
    back_mass = (
        jnp.zeros((group_count, capacity, cluster_width), jnp.float32)
        .at[back_group, ranks_here]
        .set(col_mass, mode="drop")
    )
    got_peak = lax.all_to_all(back_peak, "clusters", split_axis=0, concat_axis=0, tiled=True)
    got_mass = lax.all_to_all(back_mass, "clusters", split_axis=0, concat_axis=0, tiled=True)
    where_to = jnp.where(send_valid, send_local, per_owner).reshape(-1)
    got_peak = got_peak.reshape(group_count * capacity, cluster_width)
    got_mass = got_mass.reshape(group_count * capacity, cluster_width)
    owner_peak = (
        jnp.full((per_owner, cluster_width), sentinel, jnp.float32)
        .at[where_to]
        .max(got_peak, mode="drop")
    )
    lifted = jnp.take(owner_peak, jnp.minimum(where_to, per_owner - 1), axis=0)
    owner_mass = (
        jnp.zeros((per_owner, cluster_width), jnp.float32)
        .at[where_to]
        .add(got_mass * jnp.exp(got_peak - lifted), mode="drop")
    )
    owner_peak, owner_mass = combined_all((owner_peak, owner_mass), "tiles", lse_pair)
    reached = owner_mass > 0
    target_next = jnp.where(
        reached,
        -epsilon_reg * (owner_peak + jnp.log(jnp.where(reached, owner_mass, 1.0))),
        target_start,
    )
    source_now = source_next
    return (source_now, target_next)


def solution(mesh):
    placed = (
        P("clusters", None, "tiles"),
        P("clusters", None, None),
        P("clusters", "tiles"),
        P("clusters", None),
        P(),
        P(),
        P(),
    )
    return jax.shard_map(
        local,
        mesh=mesh,
        in_specs=placed,
        out_specs=(P("clusters", "tiles"), P("clusters", None)),
        check_vma=False,
    )
```

profile of v0, /device:TPU:6, one launch (start us, length us, event | category | flops | bytes accessed | tf_op | source)
XLA Modules:
  0.0 1596.2 jit_solution(13576200023805273357)
XLA Ops:
  1.6 80.9 %while.43 = (s32[]{:T(128)}, s32[512,12]{1,0:T(8,128)S(1)}, s32[64,2]{0,1:T(2,128)S(1)}, s32[64,8,12]{2,1,0:T(8,128)S(1)}, s32[]{:T(128)}) while((s32[]{:T(128)}, s32[512,12]{1,0:T(8,128)S(1)}, s32[64,2]{0,1:T(2,128)S(1)}, s32[64,8,12]{2,1,0:T(8,128)S(1)}, s32[]{:T(128)}) %tuple.132), condition=%wide.while_cond.1, body=%wide.while_body.1.sunk | while | flops 2 | bytes 8289 | solution.py:27
  83.3 38.6 %gather_fusion.1 = s32[6144]{0:T(1024)S(1)} fusion(s32[512]{0:T(512)S(1)} %copy-done.1, s32[6144]{0:T(1024)S(1)} %broadcast_clamp_fusion), kind=kCustom, calls=%fused_computation.3 | custom fusion | bytes 73728 | tf_op jit(solution)/shard_map/vmap(jit(_take))/gather | solution.py:30
  121.9 85.4 %while.42 = (s32[]{:T(128)}, s32[512]{0:T(512)S(1)}, s32[64,1]{0,1:T(1,128)S(1)}, s32[64,8]{1,0:T(8,128)S(1)}, s32[]{:T(128)}, /*index=5*/s32[]{:T(128)}) while((s32[]{:T(128)}, s32[512]{0:T(512)S(1)}, s32[64,1]{0,1:T(1,128)S(1)}, s32[64,8]{1,0:T(8,128)S(1)}, s32[]{:T(128)}, /*index=5*/s32[]{:T(128)}) %tuple.146), condition=%wide.while_cond, body=%wide.while_body.sunk | while | flops 2 | bytes 217 | solution.py:28
  207.6 2.3 convert_reduce_fusion
  212.8 12.0 all-to-all-start
  224.9 25.5 %gather_fusion.3 = bf16[128,30,1024]{2,0,1:T(8,128)(2,1)} fusion(bf16[8,30,1024]{2,0,1:T(8,128)(2,1)S(1)} %copy-done, s32[1024]{0:T(1024)S(1)} %pad_clamp_fusion.1), kind=kCustom, calls=%fused_computation.5 | custom fusion | bytes 15729152 | tf_op jit(solution)/shard_map/jit(_take)/gather | solution.py:99
  250.4 12.5 gather.40
  263.0 12.7 broadcast_select_fusion.5
  275.7 11.4 all-to-all-start.1
  291.4 168.2 %all-to-all-done.1 = bf16[64,2,30,1024]{3,1,2,0:T(2,128)(2,1)} async-done(((bf16[64,2,30,1024]{3,1,2,0:T(2,128)(2,1)}), bf16[64,2,30,1024]{3,1,2,0:T(2,128)(2,1)}, u32[]{:S(2)}, u32[]{:S(2)}) %all-to-all-start.1) | async-done | bytes 7864352 | tf_op jit(solution)/shard_map/all_to_all | solution.py:103
  459.6 9.3 copy.94
  468.9 9.4 gather_fusion.4
  478.3 7.9 multiply_reduce_fusion
  486.3 1028.6 %while.40 = (s32[]{:T(128)}, f32[8,256]{1,0:T(8,128)S(1)}, f32[8,256]{1,0:T(8,128)S(1)}, f32[96,1024]{1,0:T(8,128)S(1)}, f32[96,1024]{1,0:T(8,128)S(1)}, /*index...) while((s32[]{:T(128)}, f32[8,256]{1,0:T(8,128)S(1)}, ...), condition=%wide.region_10.12_spmd, body=%wide.region_5.11_spmd.sunk | while | flops 19925776 | bytes 2277753 | solution.py:154
  491.6 1.4 fusion.40
  513.0 1.4 fusion.40
  545.1 1.4 fusion.40
  577.3 1.4 fusion.40
  609.4 1.4 fusion.40
  641.6 1.4 fusion.40
  673.7 1.4 fusion.40
  705.8 1.4 fusion.40
  738.0 1.4 fusion.40
  770.1 1.4 fusion.40
  802.3 1.4 fusion.40
  834.4 1.4 fusion.40
  866.6 1.4 fusion.40
  898.7 1.4 fusion.40
  930.8 1.4 fusion.40
  963.0 1.4 fusion.40
  995.1 1.4 fusion.40
  1027.3 1.4 fusion.40
  1059.4 1.4 fusion.40
  1091.6 1.4 fusion.40
  1123.7 1.4 fusion.40
  1155.9 1.4 fusion.40
  1380.9 1.4 fusion.40
  1413.0 1.4 fusion.40
  1515.8 13.5 scatter_fusion
  1529.3 8.6 all-to-all-start.2
  1538.9 13.5 scatter_fusion.1
  1552.4 3.1 all-to-all-done.2
  1555.5 7.1 all-to-all-start.3
  1563.6 1.6 scatter_custom_fusion.1
  1565.3 12.5 all-gather
  1577.8 2.5 all-to-all-done.3
  1580.6 2.1 scatter_custom_fusion.3
  1582.7 12.7 all-gather.1
  (1892 shorter events, 789.0 us)
Async XLA Ops:
  0.6 224.3 %copy-start = (bf16[8,30,1024]{2,0,1:T(8,128)(2,1)S(1)}, bf16[8,30,1024]{2,0,1:T(8,128)(2,1)}, u32[]{:S(2)}) copy-start(bf16[8,30,1024]{2,0,1:T(8,128)(2,1)} %param.14) | copy-start | bytes 1474564
  0.6 82.6 %copy-start.1 = (s32[512]{0:T(512)S(1)}, s32[512]{0:T(512)}, u32[]{:S(2)}) copy-start(s32[512]{0:T(512)} %param.19) | copy-start | bytes 6148
  83.3 38.7 %copy-start.4 = (s32[512]{0:T(512)S(1)}, s32[512]{0:T(512)}, u32[]{:S(2)}) copy-start(s32[512]{0:T(512)} %param.18) | copy-start | bytes 6148
  83.3 127.2 %copy-start.2 = (f32[8,1024]{1,0:T(8,128)S(1)}, f32[8,1024]{1,0:T(8,128)}, u32[]{:S(2)}) copy-start(f32[8,1024]{1,0:T(8,128)} %param.16) | copy-start | bytes 98308
  212.8 62.9 %all-to-all-start = ((f32[64,2,1024]{2,1,0:T(2,128)}), f32[64,2,1024]{2,1,0:T(2,128)S(1)}, u32[]{:S(2)}, u32[]{:S(2)}) async-start(f32[64,2,1024]{2,1,0:T(2,128)} %broadcast_select_fusion.7), calls=%async_computation | async-start | bytes 1048576 | tf_op jit(solution)/shard_map/all_to_all | solution.py:115
  275.7 14.1 copy-start.3
  275.7 183.8 %all-to-all-start.1 = ((bf16[64,2,30,1024]{3,1,2,0:T(2,128)(2,1)}), bf16[64,2,30,1024]{3,1,2,0:T(2,128)(2,1)}, u32[]{:S(2)}, u32[]{:S(2)}) async-start(bf16[64,2,30,1024]{3,1,2,0:T(2,128)(2,1)} %broadcast_select_fusion.5), calls=%async_computation.1 | async-start | bytes 15728640 | tf_op jit(solution)/shard_map/all_to_all | solution.py:103
  1529.3 26.2 %all-to-all-start.2 = ((f32[64,2,1024]{2,1,0:T(2,128)}), f32[64,2,1024]{2,1,0:T(2,128)S(1)}, u32[]{:S(2)}, u32[]{:S(2)}) async-start(f32[64,2,1024]{2,1,0:T(2,128)} %scatter_fusion), calls=%async_computation.2 | async-start | bytes 1048576 | tf_op jit(solution)/shard_map/all_to_all | solution.py:167
  1555.5 24.7 %all-to-all-start.3 = ((f32[64,2,1024]{2,1,0:T(2,128)}), f32[64,2,1024]{2,1,0:T(2,128)S(1)}, u32[]{:S(2)}, u32[]{:S(2)}) async-start(f32[64,2,1024]{2,1,0:T(2,128)} %scatter_fusion.1), calls=%async_computation.3 | async-start | bytes 1048576 | tf_op jit(solution)/shard_map/all_to_all | solution.py:168
where the time goes:
time: 1620 us; the launch traced here: 1600 us
  local copies, waits for them, and re-layouts  439 us (27%)
  other arithmetic  399 us (25%)
  loops' own time  386 us (24%)
  waiting for transfers between devices  174 us (11%)
  matrix products  134 us (8%)
  starting transfers between devices  39.1 us (2%)
  blocking collectives  25.2 us (2%)
    another operation x1, loops' own time, local(): lax.fori_loop(0, slot_count, visit, start)  384 us
    all_to_all x1, waiting for transfers between devices, local(): lax.all_to_all(packed, 'clusters', split_axis=0, concat_axis=0, tiled=True)  168 us
    gather x384, local copies, waits for them, and re-layouts  165 us
    dot_general x96, matrix products, tile_stats(): lax.dot_general(points, target, (((0,), (0,)), ((), ())), preferred_eleme...  134 us
    dynamic_slice x96, other arithmetic, visit(): lax.dynamic_index_in_dim(source_now, home_cluster, 0, keepdims=False)  68 us
    select_n x96, other arithmetic, visit(): tile_row_top = jnp.where(active, tile_row_top, sentinel)  62.5 us
    select_n x96, other arithmetic, visit(): tile_row_sum = jnp.where(active, tile_row_sum, 0.0)  62.5 us
    select_n x96, other arithmetic, visit(): jnp.where(active, tile_col_top, sentinel)  62.5 us
  transfers between devices with their start and end apart: 4, of which 3 were waited for; matrix products, arithmetic and copies ran while one was open for 5% of the time, Pallas kernels for 0%

commit v1 on v0

v1 whole, which is shorter than its diff:
```python
import functools

import jax
import jax.numpy as jnp
from jax import lax
from jax.experimental import pallas as pl
from jax.experimental.pallas import tpu as pltpu
from jax.sharding import PartitionSpec as P

MESH = pl.DeviceIdType.MESH
ZS, XS, YS = 8, 4, 4
PER = 8
SHARP = 4.0
EXP2_SCALE = 5.770780163555854
LOW = -1e30
SOURCES, TARGETS = XS * 2 * PER, ZS * 2 * PER
LIST = 256
UNROLL = 8
F32, BF16, I32 = jnp.float32, jnp.bfloat16, jnp.int32


def place():
    c, y = lax.axis_index("clusters"), lax.axis_index("tiles")
    return c // 8, (c // 2) % 4, c % 2, y


def device(z, x, k, y):
    return (z * 8 + x * 2 + k, y)


def iota(shape, dim):
    return lax.broadcasted_iota(I32, shape, dim)


def widen(points, potential, work, out):
    values = points[...].astype(F32)
    half_norm = 0.5 * jnp.sum(values * values, axis=1)
    term = potential[...] - half_norm
    high = term.astype(BF16).astype(F32)
    low = (term - high).astype(BF16).astype(F32)
    work[:, 0:30, :] = values
    work[:, 30:31, :] = high[:, None, :]
    work[:, 31:32, :] = low[:, None, :]
    out(work[...].astype(BF16))
    return high + low + half_norm


def edge_list(z, x, kept, counts, home, edges_ref, has_row_ref, has_col_ref):
    lane = iota((SOURCES, 512), 1)
    row = iota((SOURCES, 512), 0)
    count = jnp.sum(jnp.where(lane == row + z * SOURCES, counts[...].astype(F32), 0.0), axis=1, keepdims=True)
    names = kept[...]
    homes = home[...].astype(F32)
    own_row = iota((SOURCES, 1), 0)
    codes, marks, before, total = [], [], [], jnp.zeros((SOURCES, 1), F32)
    for k in range(12):
        at = jnp.sum(jnp.where(names[:, k:k + 1] == lane, homes, 0.0), axis=1, keepdims=True).astype(I32)
        mark = jnp.where((count > float(k)) & (((at >> 4) & 3) == x), 1.0, 0.0)
        codes.append((own_row * TARGETS + ((at >> 6) << 4) + (at & 15) + 1).astype(F32))
        marks.append(mark)
        before.append(total)
        total = total + mark
    square_row, square_lane = iota((SOURCES, SOURCES), 0), iota((SOURCES, SOURCES), 1)
    across = jnp.sum(jnp.where(square_row == square_lane, total, 0.0), axis=0, keepdims=True)
    ahead = jnp.sum(jnp.where(square_lane < square_row, across, 0.0), axis=1, keepdims=True)
    slot = iota((SOURCES, LIST), 1).astype(F32)
    filled = jnp.zeros((SOURCES, LIST), F32)
    for code, mark, prior in zip(codes, marks, before):
        filled = filled + jnp.where((slot == ahead + prior) & (mark > 0.0), code, 0.0)
    listed = jnp.sum(filled, axis=0, keepdims=True)
    number = jnp.sum(total, axis=0, keepdims=True)
    chosen = jnp.where(listed > 0.0, listed - 1.0, float(SOURCES * TARGETS)).astype(I32)
    edges_ref[...] = jnp.where(iota((8, LIST), 0) == 0, chosen, number.astype(I32))
    has_row_ref[...] = jnp.broadcast_to(jnp.where(total > 0.0, 1.0, 0.0), has_row_ref.shape)
    named = (iota((TARGETS, LIST), 0) == (chosen & (TARGETS - 1))) & (listed > 0.0)
    has_col_ref[...] = jnp.broadcast_to(
        jnp.max(jnp.where(named, 1.0, 0.0), axis=1, keepdims=True), has_col_ref.shape)


def collect_kernel(sp_hbm, tp_hbm, f_hbm, g_hbm, kept_hbm, counts_hbm, home_hbm,
                   src, turned, edges_ref, has_row_ref, has_col_ref, src_base, tgt_base, kept_pot,
                   sp, tp, f, g, kept, counts, home, work, spare, tgt,
                   load_sem, send_sem, recv_sem):
    z, x, k, y = place()
    step = lambda at, by, n: lax.rem(at + (by + n), n)

    loads = [
        pltpu.make_async_copy(a, b, load_sem.at[i])
        for i, (a, b) in enumerate([
            (sp_hbm, sp),
            (f_hbm, f),
            (tp_hbm.at[:, :, pl.ds(pl.multiple_of(y * 256, 256), 256)], tp),
            (g_hbm.at[:, pl.ds(pl.multiple_of(y * 256, 256), 256)], g),
            (kept_hbm.at[pl.ds(pl.multiple_of(z * SOURCES, SOURCES), SOURCES), :], kept),
            (counts_hbm, counts),
            (home_hbm, home),
        ])
    ]
    for load in loads:
        load.start()

    mate = device(z, x, 1 - k, y)
    xn = {d: device(z, step(x, d, XS), k, y) for d in (1, -1)}
    yn = {d: device(z, x, k, step(y, d, YS)) for d in (1, -1)}
    zn = {d: device(step(z, d, ZS), x, k, y) for d in (1, -1)}

    barrier = pltpu.get_barrier_semaphore()
    for other in (mate, xn[1], xn[-1], yn[1], yn[-1], zn[1], zn[-1]):
        pl.semaphore_signal(barrier, inc=1, device_id=other, device_id_type=MESH)

    numbers = {}
    pending = []

    def descriptor(key, ref, to):
        m = numbers.setdefault(key, len(numbers))
        return pltpu.make_async_remote_copy(
            src_ref=ref, dst_ref=ref, send_sem=send_sem.at[m], recv_sem=recv_sem.at[m],
            device_id=to, device_id_type=MESH)

    def send(key, ref, to):
        copy = descriptor(key, ref, to)
        copy.start()
        pending.append(copy)

    def arrive(key, ref):
        descriptor(key, ref, mate).wait_recv()

    def src_block(dx, dy, q, lo=0, n=PER):
        return src.at[step(y, dy, YS), pl.ds(step(x, dx, XS) * 16 + q * 8 + lo, n)]

    loads[0].wait()
    loads[1].wait()

    def put_source(block):
        halves = block[:, :, 0:128], block[:, :, 128:256]
        src[y, pl.ds(x * 16 + k * 8, PER)] = jnp.where(k == 0, halves[0], halves[1])
        spare[...] = jnp.where(k == 0, halves[1], halves[0])

    src_base[...] = widen(sp, f, work, put_source)
    pl.semaphore_wait(barrier, 7)
    cross = pltpu.make_async_remote_copy(
        src_ref=spare, dst_ref=src.at[y, pl.ds(x * 16 + k * 8, PER)],
        send_sem=send_sem.at[numbers.setdefault("cross", len(numbers))],
        recv_sem=recv_sem.at[numbers["cross"]], device_id=mate, device_id_type=MESH)
    cross.start()
    pending.append(cross)

    loads[2].wait()
    loads[3].wait()

    def put_target(block):
        tgt[z, k] = block

    tgt_base[...] = widen(tp, g, work, put_target)
    kept_pot[...] = g[...]

    def tgt_chunk(dz, c, core):
        return tgt.at[step(z, dz, ZS), core, pl.ds(c * 4, 4)]

    wide_id = iota((32, 256), 0)
    tail_id = iota((16, 256), 0)

    def turn(dz, c, core):
        zz = step(z, dz, ZS)

        def one(i, _):
            block = tgt[zz, core, c * 4 + i].astype(F32)
            top = jnp.where(wide_id < 30, block, 1.0)
            low = jnp.where(tail_id >= 14, block[16:32], 0.0)
            turned[zz * 16 + core * 8 + c * 4 + i] = jnp.concatenate([top, low], axis=0).T.astype(BF16)
            return 0

        lax.fori_loop(0, 4, one, 0, unroll=4)

    def pass_target(dz, c, forward):
        for d in forward:
            send(("z", d, dz, c), tgt_chunk(dz, c, k), zn[d])
        send(("m", dz, c), tgt_chunk(dz, c, k), mate)

    def take_target(d, dz, c, forward):
        arrive(("z", d, dz + d, c), tgt_chunk(dz, c, k))
        for e in forward:
            send(("z", e, dz, c), tgt_chunk(dz, c, k), zn[e])
        send(("m", dz, c), tgt_chunk(dz, c, k), mate)

    def take_mate(dz, c):
        arrive(("m", dz, c), tgt_chunk(dz, c, 1 - k))
        turn(dz, c, 1 - k)

    def off(q, first, second):
        return (first, second) if q == 0 else (second, first)

    near = {0: (xn, yn), 1: (yn, xn)}

    def first_out(q):
        for d in (1, -1):
            send(("a", q, d), src_block(0, 0, q), near[q][0][d])

    def first_in(q, d):
        dx, dy = off(q, -d, 0)
        arrive(("a", q, d), src_block(dx, dy, q))
        lo = 0 if d == 1 else 4
        send(("af", q, d), src_block(dx, dy, q, lo, 4), near[q][0][d])

    def first_far(q):
        dx, dy = off(q, 2, 0)
        for d in (1, -1):
            arrive(("af", q, d), src_block(dx, dy, q, 0 if d == 1 else 4, 4))

    def second_out(q, e):
        dx, dy = off(q, e, 0)
        for d in (1, -1):
            send(("b", q, e, d), src_block(dx, dy, q), near[q][1][d])

    def second_in(q, e):
        for d in (1, -1):
            dx, dy = off(q, e, -d)
            arrive(("b", q, e, d), src_block(dx, dy, q))
            send(("bf", q, e, d), src_block(dx, dy, q, 0 if d == 1 else 4, 4), near[q][1][d])

    def second_far(q, e):
        dx, dy = off(q, e, 2)
        for d in (1, -1):
            arrive(("bf", q, e, d), src_block(dx, dy, q, 0 if d == 1 else 4, 4))

    for c, d in ((0, 1), (1, -1)):
        send(("z", d, 0, c), tgt_chunk(0, c, k), zn[d])
    for c, d in ((1, 1), (0, -1)):
        send(("z", d, 0, c), tgt_chunk(0, c, k), zn[d])
    pltpu.make_async_remote_copy(
        src_ref=spare, dst_ref=src.at[y, pl.ds(x * 16 + (1 - k) * 8, PER)],
        send_sem=send_sem.at[numbers["cross"]], recv_sem=recv_sem.at[numbers["cross"]],
        device_id=mate, device_id_type=MESH).wait_recv()
    for q in (0, 1):
        first_out(q)
    for q in (0, 1):
        second_out(q, 0)
    for c in (0, 1):
        send(("m", 0, c), tgt_chunk(0, c, k), mate)
    for load in loads[4:]:
        load.wait()
    edge_list(z, x, kept, counts, home, edges_ref, has_row_ref, has_col_ref)
    idle = iota((32, 128), 0)
    for at in range(YS):
        src[at, SOURCES] = jnp.where(idle == 30, LOW, 0.0).astype(BF16)

    take_target(1, -1, 0, (1,))
    take_target(-1, 1, 1, (-1,))
    for q in (0, 1):
        for d in (1, -1):
            first_in(q, d)
        for e in (-1, 1):
            second_out(q, e)
    for c in (0, 1):
        turn(0, c, k)
    take_target(1, -1, 1, (1,))
    take_target(-1, 1, 0, (-1,))
    for q in (0, 1):
        second_in(q, 0)
    turn(-1, 0, k)
    turn(1, 1, k)
    take_mate(0, 0)
    take_mate(0, 1)
    take_target(1, -2, 0, (1,))
    take_target(-1, 2, 1, (-1,))
    for q in (0, 1):
        first_far(q)
        second_out(q, 2)
    turn(-1, 1, k)
    turn(1, 0, k)
    take_mate(-1, 0)
    take_mate(1, 1)
    take_target(1, -2, 1, (1,))
    take_target(-1, 2, 0, (-1,))
    for q in (0, 1):
        second_in(q, -1)
    turn(-2, 0, k)
    turn(2, 1, k)
    take_mate(-1, 1)
    take_mate(1, 0)
    take_target(1, -3, 0, (1,))
    take_target(-1, 3, 1, (-1,))
    for q in (0, 1):
        second_in(q, 1)
    turn(-2, 1, k)
    turn(2, 0, k)
    take_mate(-2, 0)
    take_mate(2, 1)
    take_target(1, -3, 1, ())
    take_target(-1, 3, 0, ())
    for q in (0, 1):
        second_in(q, 2)
    turn(-3, 0, k)
    turn(3, 1, k)
    take_mate(-2, 1)
    take_mate(2, 0)
    take_target(1, -4, 0, ())
    take_target(-1, 4, 1, ())
    turn(-3, 1, k)
    turn(3, 0, k)
    take_mate(-3, 0)
    take_mate(3, 1)
    turn(-4, 0, k)
    turn(4, 1, k)
    take_mate(-3, 1)
    take_mate(3, 0)
    take_mate(-4, 0)
    take_mate(4, 1)
    for q in (0, 1):
        for e in (0, -1, 1, 2):
            second_far(q, e)
    for copy in pending:
        copy.wait_send()


MESSAGES = 96


def collect(sp, tp, f, g, kept, counts, home):
    anyspace = pl.BlockSpec(memory_space=pl.ANY)
    vmem = pl.BlockSpec(memory_space=pltpu.VMEM)
    shape = jax.ShapeDtypeStruct
    return pl.pallas_call(
        collect_kernel,
        out_shape=(
            shape((YS, SOURCES + 1, 32, 128), BF16),
            shape((TARGETS, 256, 48), BF16),
            shape((8, LIST), I32),
            shape((SOURCES, 128), F32),
            shape((TARGETS, 128), F32),
            shape((PER, 256), F32),
            shape((PER, 256), F32),
            shape((PER, 256), F32),
        ),
        in_specs=[anyspace] * 7,
        out_specs=(vmem,) * 8,
        scratch_shapes=[
            pltpu.VMEM((PER, 30, 256), BF16),
            pltpu.VMEM((PER, 30, 256), BF16),
            pltpu.VMEM((PER, 256), F32),
            pltpu.VMEM((PER, 256), F32),
            pltpu.VMEM((SOURCES, 12), I32),
            pltpu.VMEM((1, 512), I32),
            pltpu.VMEM((1, 512), I32),
            pltpu.VMEM((PER, 32, 256), F32),
            pltpu.VMEM((PER, 32, 128), BF16),
            pltpu.VMEM((ZS, 2, PER, 32, 256), BF16),
            pltpu.SemaphoreType.DMA((7,)),
            pltpu.SemaphoreType.DMA((MESSAGES,)),
            pltpu.SemaphoreType.DMA((MESSAGES,)),
        ],
        compiler_params=pltpu.CompilerParams(
            collective_id=0, has_side_effects=True, vmem_limit_bytes=32 * 2**20),
        name="collect",
    )(sp, tp, f, g, kept, counts, home)


def tiles_kernel(edge_vmem, src, turned, has_row_ref, has_col_ref, row_ref, col_ref,
                 edge_ref, row_acc, col_acc, edge_sem):
    load = pltpu.make_async_copy(edge_vmem, edge_ref, edge_sem)
    load.start()
    width = turned.shape[1]
    tail = jnp.where(iota((16, YS * 128), 0) >= 14, 1.0, 0.0).astype(BF16)
    row_acc[...] = jnp.zeros(row_acc.shape, F32)
    col_acc[...] = jnp.zeros(col_acc.shape, F32)
    load.wait()
    count = edge_ref[1, 0]

    def scores(s, p):
        cells = jnp.concatenate([src[at, s] for at in range(YS)], axis=1)
        right = jnp.concatenate([cells, tail], axis=0)
        return jnp.dot(turned[p], right, preferred_element_type=F32)

    def step(it, _):
        got = []
        for u in range(UNROLL):
            code = edge_ref[0, it * UNROLL + u]
            s, p = code // TARGETS, code % TARGETS
            e = jnp.exp2(scores(s, p) * EXP2_SCALE)
            rows = e.reshape(width // 8, 8, YS * 128).sum(axis=0)
            q = (e[:, 0:128] + e[:, 128:256]) + (e[:, 256:384] + e[:, 384:512])
            got.append((s, p, rows, q.T.reshape(16, 8, width).sum(axis=0)))
        for s, p, rows, cols in got:
            row_acc[s] += rows
            col_acc[p] += cols
        return 0

    lax.fori_loop(0, (count + UNROLL - 1) // UNROLL, step, 0)

    row_sum = jnp.sum(row_acc[0:SOURCES], axis=1)
    col_sum = jnp.sum(col_acc[...], axis=1)
    has_row = has_row_ref[:, 0:1] > 0.0
    has_col = has_col_ref[:, 0:1] > 0.0

    def outside(has, total):
        good = (total >= 2.0**-90) & (total <= 2.0**120)
        return jnp.max(jnp.where(has & jnp.logical_not(good), 1.0, 0.0))

    row_ref[...] = jnp.where(has_row, jnp.log(jnp.where(has_row, row_sum, 1.0)), LOW)
    col_ref[...] = jnp.where(has_col, jnp.log(jnp.where(has_col, col_sum, 1.0)), LOW)
    spread = jnp.maximum(outside(has_row, row_sum), outside(has_col, col_sum))

    @pl.when(spread > 0.0)
    def _():
        row_ref[...] = jnp.full(row_ref.shape, LOW, F32)
        col_ref[...] = jnp.full(col_ref.shape, LOW, F32)

        def merge(values, ref, at):
            top = jnp.max(values, axis=0, keepdims=True)
            here = top + jnp.log(jnp.sum(jnp.exp(values - top), axis=0, keepdims=True))
            old = ref[pl.ds(at, 1), :]
            peak = jnp.maximum(here, old)
            ref[pl.ds(at, 1), :] = peak + jnp.log(jnp.exp(here - peak) + jnp.exp(old - peak))

        def careful(e, _):
            code = edge_ref[0, e]
            s, p = code // TARGETS, code % TARGETS
            value = SHARP * scores(s, p)
            merge(value, row_ref, s)
            merge(value.T, col_ref, p)
            return 0

        lax.fori_loop(0, count, careful, 0)


def tiles(edges, src, turned, has_row, has_col):
    vmem = pl.BlockSpec(memory_space=pltpu.VMEM)
    shape = jax.ShapeDtypeStruct
    return pl.pallas_call(
        tiles_kernel,
        out_shape=(shape((SOURCES, YS * 128), F32), shape((TARGETS, 256), F32)),
        in_specs=[vmem] * 5,
        out_specs=(vmem, vmem),
        scratch_shapes=[
            pltpu.SMEM((8, LIST), I32),
            pltpu.VMEM((SOURCES + 1, 8, YS * 128), F32),
            pltpu.VMEM((TARGETS, 8, 256), F32),
            pltpu.SemaphoreType.DMA,
        ],
        compiler_params=pltpu.CompilerParams(vmem_limit_bytes=32 * 2**20),
        name="tiles",
    )(edges, src, turned, has_row, has_col)


def log_sum(parts):
    top = functools.reduce(jnp.maximum, parts)
    return top + jnp.log(sum(jnp.exp(part - top) for part in parts))


def settle_kernel(row, col, src_base, tgt_base, kept_pot, src_out, tgt_out,
                  row_y, row_x, row_k, col_k, col_z, wide, row_mid, row_end, col_mid,
                  send_sem, recv_sem):
    z, x, k, y = place()
    turn = lambda at, by, n: lax.rem(at + by, n)
    mate = device(z, x, 1 - k, y)
    xs = [device(z, turn(x, d, XS), k, y) for d in range(1, XS)]
    ys = [device(z, x, k, turn(y, d, YS)) for d in range(1, YS)]
    zs = [device(turn(z, d, ZS), x, k, y) for d in range(1, ZS)]
    barrier = pltpu.get_barrier_semaphore()
    everyone = [mate] + xs + ys + zs
    for other in everyone:
        pl.semaphore_signal(barrier, inc=1, device_id=other, device_id_type=MESH)
    pl.semaphore_wait(barrier, len(everyone))
    used = [0]

    def send(src_ref, dst_ref, to):
        m = used[0]
        used[0] += 1
        copy = pltpu.make_async_remote_copy(
            src_ref=src_ref, dst_ref=dst_ref, send_sem=send_sem.at[m], recv_sem=recv_sem.at[m],
            device_id=to, device_id_type=MESH)
        copy.start()
        return copy

    first = [send(row.at[:, pl.ds(pl.multiple_of(turn(y, d, YS) * 128, 128), 128)], row_y.at[d - 1], ys[d - 1])
             for d in range(1, YS)]
    first.append(send(col.at[:, 1 - k], col_k, mate))
    own_row = row[:, pl.ds(pl.multiple_of(y * 128, 128), 128)]
    for copy in first:
        copy.wait_recv()
    row_mid[...] = log_sum([own_row] + [row_y[d] for d in range(YS - 1)]).reshape(row_mid.shape)
    col_mid[...] = log_sum([col[:, k], col_k[...]])

    second = [send(row_mid.at[turn(x, d, XS)], row_x.at[d - 1], xs[d - 1]) for d in range(1, XS)]
    second += [send(col_mid.at[turn(z, d, ZS)], col_z.at[d - 1], zs[d - 1]) for d in range(1, ZS)]
    for copy in second:
        copy.wait_recv()
    row_end[...] = log_sum([row_mid[x]] + [row_x[d] for d in range(XS - 1)])
    total = log_sum([col_mid[z]] + [col_z[d] for d in range(ZS - 1)])
    result = jnp.where(total > 0.5 * LOW, -0.25 * total + tgt_base[...], kept_pot[...])
    wide[y] = result

    third = [send(row_end.at[1 - k], row_k, mate)]
    third += [send(wide.at[y], wide.at[y], ys[d - 1]) for d in range(1, YS)]
    third[0].wait_recv()
    halves = row_end[k], row_k[...]
    base = src_base[...]
    src_out[:, 0:128] = base[:, 0:128] - 0.25 * jnp.where(k == 0, halves[0], halves[1])
    src_out[:, 128:256] = base[:, 128:256] - 0.25 * jnp.where(k == 0, halves[1], halves[0])
    for d in range(1, YS):
        m = used[0] - YS + d
        pltpu.make_async_remote_copy(
            src_ref=wide.at[turn(y, YS - d, YS)], dst_ref=wide.at[turn(y, YS - d, YS)],
            send_sem=send_sem.at[m], recv_sem=recv_sem.at[m],
            device_id=mate, device_id_type=MESH).wait_recv()
    for at in range(YS):
        tgt_out[:, at * 256:(at + 1) * 256] = wide[at]
    for copy in first + second + third:
        copy.wait_send()


def settle(row, col, src_base, tgt_base, kept_pot):
    vmem = pl.BlockSpec(memory_space=pltpu.VMEM)
    shape = jax.ShapeDtypeStruct
    return pl.pallas_call(
        settle_kernel,
        out_shape=(shape((PER, 256), F32), shape((PER, 1024), F32)),
        in_specs=[vmem] * 5,
        out_specs=(vmem, vmem),
        scratch_shapes=[
            pltpu.VMEM((YS - 1, SOURCES, 128), F32),
            pltpu.VMEM((XS - 1, 2, PER, 128), F32),
            pltpu.VMEM((PER, 128), F32),
            pltpu.VMEM((ZS, PER, 256), F32),
            pltpu.VMEM((ZS - 1, PER, 256), F32),
            pltpu.VMEM((YS, PER, 256), F32),
            pltpu.VMEM((XS, 2, PER, 128), F32),
            pltpu.VMEM((2, PER, 128), F32),
            pltpu.VMEM((ZS, PER, 256), F32),
            pltpu.SemaphoreType.DMA((24,)),
            pltpu.SemaphoreType.DMA((24,)),
        ],
        compiler_params=pltpu.CompilerParams(
            collective_id=1, has_side_effects=True, vmem_limit_bytes=32 * 2**20),
        name="settle",
    )(row, col.reshape(ZS, 2, PER, 256), src_base, tgt_base, kept_pot)


def local(sp, tp, f, g, kept, counts, home):
    src, turned, edges, has_row, has_col, src_base, tgt_base, kept_pot = collect(
        sp, tp, f, g, kept, counts.reshape(1, -1), home.reshape(1, -1))
    row, col = tiles(edges, src, turned, has_row, has_col)
    return settle(row, col, src_base, tgt_base, kept_pot)


def solution(mesh):
    placed = (
        P("clusters", None, "tiles"),
        P("clusters", None, None),
        P("clusters", "tiles"),
        P("clusters", None),
        P(),
        P(),
        P(),
    )
    return jax.shard_map(
        local,
        mesh=mesh,
        in_specs=placed,
        out_specs=(P("clusters", "tiles"), P("clusters", None)),
        check_vma=False,
    )
```

time: 1620 us -> 139 us (0.09); the launches traced: 1600 us -> 137 us
  local copies, waits for them, and re-layouts: 439 us -> 7.15 us
  other arithmetic: 399 us -> 0 us
  loops' own time: 386 us -> 0 us
  waiting for transfers between devices: 174 us -> 0 us
  matrix products: 134 us -> 0 us
  Pallas kernels: 0 us -> 129 us
  starting transfers between devices: 39.1 us -> 0 us
  blocking collectives: 25.2 us -> 0 us
    another operation x4 -> x0, loops' own time: 386 us -> none  [the longest x1 384 us: local(): lax.fori_loop(0, slot_count, visit, start)]
    select_n x395 -> x0, other arithmetic: 264 us -> none  [the longest x96 62.5 us: visit(): tile_row_top = jnp.where(active, tile_row_top, sentinel)]
    gather x393 -> x0, local copies, waits for them, and re-layouts: 253 us -> none
    all_to_all x4 -> x0, waiting for transfers between devices: 174 us -> none  [the longest x1 168 us: local(): lax.all_to_all(packed, 'clusters', split_axis=0, concat_axis=0, tiled=True)]
    dot_general x96 -> x0, matrix products: 134 us -> none  [tile_stats(): lax.dot_general(points, target, (((0,), (0,)), ((), ())), preferred_eleme...]
    pallas_call x0 -> x3, Pallas kernels: none -> 129 us  [the longest x1 71.7 us: tiles(): pl.pallas_call(tiles_kernel, out_shape=(shape((SOURCES, YS * 128), F32),...]
    dynamic_slice x195 -> x0, local copies, waits for them, and re-layouts: 114 us -> none  [the longest x96 56.7 us: visit(): active = living[slot_at]]
    dynamic_slice x96 -> x0, other arithmetic: 68 us -> none  [visit(): lax.dynamic_index_in_dim(source_now, home_cluster, 0, keepdims=False)]
  transfers between devices with their start and end apart: 4 -> 0, of which waited for: 3 -> 0; matrix products, arithmetic and copies ran while one was open for 5% -> 0% of each run, Pallas kernels for 0% -> 0%
where the time goes in v1:
time: 139 us; the launch traced here: 137 us
  Pallas kernels  129 us (93%)
  local copies, waits for them, and re-layouts  7.15 us (5%)
    pallas_call x1, Pallas kernels, tiles(): pl.pallas_call(tiles_kernel, out_shape=(shape((SOURCES, YS * 128), F32),...  71.7 us
    pallas_call x1, Pallas kernels, settle(): pl.pallas_call(settle_kernel, out_shape=(shape((PER, 256), F32), shape((P...  29 us
    pallas_call x1, Pallas kernels, collect(): pl.pallas_call(collect_kernel, out_shape=(shape((YS, SOURCES + 1, 32, 128...  28.6 us
    unnamed x13, local copies, waits for them, and re-layouts  7.15 us

profile of v1, /device:TPU:6, one launch (start us, length us, event | category | flops | bytes accessed | tf_op | source)
XLA Modules:
  0.0 137.1 jit_solution(3541498895325166016)
XLA Ops:
  0.6 0.9 copy.9.sp_hbm
  1.6 0.9 copy.11.kept_hbm
  2.5 1.3 copy.10.tp_hbm
  3.8 0.0 copy-start
  3.8 0.7 copy-done
  4.5 0.0 copy-start.1
  4.5 0.7 copy-done.1
  5.2 0.0 copy-start.2
  5.2 0.7 copy-done.2
  5.9 0.0 copy-start.3
  5.9 0.7 copy-done.3
  6.6 28.6 %collect.1 = (bf16[4,65,32,128]{3,2,1,0:T(8,128)(2,1)S(1)}, bf16[128,256,48]{2,1,0:T(8,128)(2,1)S(1)}, s32[8,256]{1,0:T(8,128)S(1)}, f32[64,128]{1,0:T(8,128)S(1...) custom-call(bf16[8,30,256]{2,1,0:T(8,128)(2,1)S(1)} %copy.9.sp_hbm, ...), custom_call_target="tpu_custom_call" | custom-call | tf_op jit(solution)/shard_map/collect/pallas_call | solution.py:323
  35.2 71.7 %tiles.1 = (f32[64,512]{1,0:T(8,128)S(1)}, f32[128,256]{1,0:T(8,128)S(1)}) custom-call(s32[8,256]{1,0:T(8,128)S(1)} %get-tuple-element.12.edge_vmem, bf16[4,65,32,128]{3,2,1,0:T(8,128)(2,1)S(1)} %get-tuple-element.13.src, bf16[128,256,48]{2,1,0:T(8,128)(2,1)S(1)} %get-tuple-element.14.turned, f32[64,128]{1,0:T(8,128)S(1)} %get-tuple-element.15.has_row_ref, ...), custom_call_target="tpu_custom_call" | custom-call | tf_op jit(solution)/shard_map/tiles/pallas_call | solution.py:429
  106.9 29.0 %settle.1 = (f32[8,256]{1,0:T(8,128)S(1)}, f32[8,1024]{1,0:T(8,128)S(1)}) custom-call(f32[64,512]{1,0:T(8,128)S(1)} %get-tuple-element.17.row, f32[8,2,8,256]{3,2,1,0:T(8,128)S(1)} %bitcast.3, f32[8,256]{1,0:T(8,128)S(1)} %get-tuple-element.19.src_base, f32[8,256]{1,0:T(8,128)S(1)} %get-tuple-element.20.tgt_base, f32[8,256]{1,0:T(8,128)S(1)} %get-tuple-element.21.kept_pot), custom_call_target="tpu_custom_call" | custom-call | tf_op jit(solution)/shard_map/settle/pallas_call | solution.py:515
  135.8 0.6 copy.14
  136.4 0.6 copy.15
Async XLA Ops:
  3.8 0.8 copy-start
  4.5 0.7 copy-start.1
  5.2 0.7 copy-start.2
  5.9 0.7 copy-start.3

commit v2 on v1

v2 whole, which is shorter than its diff:
```python
import functools

import jax
import jax.numpy as jnp
from jax import lax
from jax.experimental import pallas as pl
from jax.experimental.pallas import tpu as pltpu
from jax.sharding import PartitionSpec as P

MESH = pl.DeviceIdType.MESH
ZS, XS, YS = 8, 4, 4
PER = 8
SHARP = 4.0
EXP2_SCALE = 5.770780163555854
LOW = -1e30
SOURCES, TARGETS = XS * 2 * PER, ZS * 2 * PER
LIST = 256
CHUNK = 2
EARLY = 1
WIDE, SLIM = 32, 8
F32, BF16, I32 = jnp.float32, jnp.bfloat16, jnp.int32


def place():
    c, y = lax.axis_index("clusters"), lax.axis_index("tiles")
    return c // 8, (c // 2) % 4, c % 2, y


def device(z, x, k, y):
    return (z * 8 + x * 2 + k, y)


def iota(shape, dim):
    return lax.broadcasted_iota(I32, shape, dim)


def widen(points, potential, out):
    values = points.astype(F32)
    half_norm = 0.5 * jnp.sum(values * values, axis=0)
    term = potential - half_norm
    high = term.astype(BF16).astype(F32)
    low = (term - high).astype(BF16).astype(F32)
    full = jnp.concatenate([values, high[None], low[None]], axis=0)
    out(jnp.swapaxes(full, 0, 1).astype(BF16))
    return high + low + half_norm


def edge_list(z, x, kept, counts, home, edges_ref, has_row_ref, has_col_ref):
    lane = iota((SOURCES, 512), 1)
    row = iota((SOURCES, 512), 0)
    mine = lane == row + z * SOURCES
    count = jnp.sum(jnp.where(mine, counts[...].astype(F32), 0.0), axis=1, keepdims=True)
    names = kept[...].astype(F32)
    lane = lane.astype(F32)
    homes = home[...].astype(F32)
    own_row = iota((SOURCES, 1), 0)
    codes, marks, before, total = [], [], [], jnp.zeros((SOURCES, 1), F32)
    for k in range(12):
        name = jnp.sum(jnp.where(mine, names[k:k + 1], 0.0), axis=1, keepdims=True)
        at = jnp.sum(jnp.where(name == lane, homes, 0.0), axis=1, keepdims=True).astype(I32)
        mark = jnp.where((count > float(k)) & (((at >> 4) & 3) == x), 1.0, 0.0)
        codes.append((own_row * TARGETS + ((at >> 6) << 4) + (at & 15) + 1).astype(F32))
        marks.append(mark)
        before.append(total)
        total = total + mark
    square_row, square_lane = iota((SOURCES, SOURCES), 0), iota((SOURCES, SOURCES), 1)
    across = jnp.sum(jnp.where(square_row == square_lane, total, 0.0), axis=0, keepdims=True)
    ahead = jnp.sum(jnp.where(square_lane < square_row, across, 0.0), axis=1, keepdims=True)
    slot = iota((SOURCES, LIST), 1).astype(F32)
    filled = jnp.zeros((SOURCES, LIST), F32)
    for code, mark, prior in zip(codes, marks, before):
        filled = filled + jnp.where((slot == ahead + prior) & (mark > 0.0), code, 0.0)
    listed = jnp.sum(filled, axis=0, keepdims=True)
    number = jnp.sum(total, axis=0, keepdims=True)
    chosen = jnp.where(listed > 0.0, listed - 1.0, float(SOURCES * TARGETS)).astype(I32)
    edges_ref[...] = jnp.where(iota((8, LIST), 0) == 0, chosen, number.astype(I32))
    has_row_ref[...] = jnp.broadcast_to(jnp.where(total > 0.0, 1.0, 0.0), has_row_ref.shape)
    named = (iota((TARGETS, LIST), 0) == (chosen & (TARGETS - 1))) & (listed > 0.0)
    has_col_ref[...] = jnp.broadcast_to(
        jnp.max(jnp.where(named, 1.0, 0.0), axis=1, keepdims=True), has_col_ref.shape)


def idle_kernel(out):
    out[...] = jnp.where(iota(out.shape, 0) == 30, LOW, 0.0)


def idle_source():
    return pl.pallas_call(
        idle_kernel,
        out_shape=jax.ShapeDtypeStruct((32, 128), F32),
        out_specs=pl.BlockSpec(memory_space=pltpu.VMEM),
        name="idle",
        cost_estimate=pl.CostEstimate(flops=10**10, bytes_accessed=10**7, transcendentals=0),
    )()


def collect_kernel(idle, sp, tp, f, g, kept, counts, home,
                   src, turned, edges_ref, has_row_ref, has_col_ref, src_base, tgt_base, kept_pot,
                   spare, tgt, send_sem, recv_sem):
    z, x, k, y = place()
    step = lambda at, by, n: lax.rem(at + (by + n), n)

    mate = device(z, x, 1 - k, y)
    xn = {d: device(z, step(x, d, XS), k, y) for d in (1, -1, 2)}
    yn = {d: device(z, x, k, step(y, d, YS)) for d in (1, -1, 2)}
    zn = {d: device(step(z, d, ZS), x, k, y) for d in (1, -1)}

    barrier = pltpu.get_barrier_semaphore()
    for other in (mate, *xn.values(), *yn.values(), *zn.values()):
        pl.semaphore_signal(barrier, inc=1, device_id=other, device_id_type=MESH)

    numbers = {}
    pending = []

    def descriptor(key, ref, to):
        m = numbers.setdefault(key, len(numbers))
        return pltpu.make_async_remote_copy(
            src_ref=ref, dst_ref=ref, send_sem=send_sem.at[m], recv_sem=recv_sem.at[m],
            device_id=to, device_id_type=MESH)

    def send(key, ref, to):
        copy = descriptor(key, ref, to)
        copy.start()
        pending.append(copy)

    def arrive(key, ref):
        descriptor(key, ref, mate).wait_recv()

    def src_block(dx, dy, q, lo=0, n=PER):
        return src.at[step(y, dy, YS), pl.ds(step(x, dx, XS) * 16 + q * 8 + lo, n)]


    def put_target(block):
        tgt[z, k] = block

    quarter = pl.ds(pl.multiple_of(y * 256, 256), 256)
    tgt_base[...] = widen(tp[:, :, quarter], g[:, quarter], put_target)
    kept_pot[...] = g[:, quarter]
    pl.semaphore_wait(barrier, 9)

    def tgt_chunk(dz, c, core):
        return tgt.at[step(z, dz, ZS), core, pl.ds(c * CHUNK, CHUNK)]

    wide_id = iota((32, 256), 0)
    tail_id = iota((16, 256), 0)

    def turn(dz, c, core):
        zz = step(z, dz, ZS)

        def one(i, _):
            block = tgt[zz, core, c * CHUNK + i].astype(F32)
            top = jnp.where(wide_id < 30, block, 1.0)
            low = jnp.where(tail_id >= 14, block[16:32], 0.0)
            turned[zz * 16 + core * 8 + c * CHUNK + i] = jnp.concatenate([top, low], axis=0).T.astype(BF16)
            return 0

        lax.fori_loop(0, CHUNK, one, 0, unroll=CHUNK)

    def take_target(d, dz, c, forward):
        arrive(("z", d, dz + d, c), tgt_chunk(dz, c, k))
        for e in forward:
            send(("z", e, dz, c), tgt_chunk(dz, c, k), zn[e])
        send(("m", dz, c), tgt_chunk(dz, c, k), mate)

    def take_mate(dz, c):
        arrive(("m", dz, c), tgt_chunk(dz, c, 1 - k))
        turn(dz, c, 1 - k)

    def off(q, first, second):
        return (first, second) if q == 0 else (second, first)

    near = {0: (xn, yn), 1: (yn, xn)}

    def first_out(q):
        for d in (1, -1, 2):
            send(("a", q, d), src_block(0, 0, q), near[q][0][d])

    def first_in(q, d):
        arrive(("a", q, d), src_block(*off(q, -d, 0), q))

    def second_out(q, e):
        for d in (1, -1) if e != 2 else (2, 1, -1):
            send(("b", q, e, d), src_block(*off(q, e, 0), q), near[q][1][d])

    def second_in(q, e):
        for d in (1, -1):
            dx, dy = off(q, e, -d)
            arrive(("b", q, e, d), src_block(dx, dy, q))
            if e != 2:
                send(("bf", q, e, d), src_block(dx, dy, q, 0 if d == 1 else 4, 4), near[q][1][d])

    def second_far(q, e):
        dx, dy = off(q, e, 2)
        if e == 2:
            arrive(("b", q, e, 2), src_block(dx, dy, q))
            return
        for d in (1, -1):
            arrive(("bf", q, e, d), src_block(dx, dy, q, 0 if d == 1 else 4, 4))

    def put_source(block):
        halves = block[:, :, 0:128], block[:, :, 128:256]
        src[y, pl.ds(x * 16 + k * 8, PER)] = jnp.where(k == 0, halves[0], halves[1])
        spare[...] = jnp.where(k == 0, halves[1], halves[0])

    chunks = PER // CHUNK
    up = tuple(range(chunks))
    down = up[::-1]

    for c, e in zip(up, down):
        send(("z", 1, 0, c), tgt_chunk(0, c, k), zn[1])
        send(("z", -1, 0, e), tgt_chunk(0, e, k), zn[-1])
    src_base[...] = widen(sp[...], f[...], put_source)
    cross = pltpu.make_async_remote_copy(
        src_ref=spare, dst_ref=src.at[y, pl.ds(x * 16 + k * 8, PER)],
        send_sem=send_sem.at[numbers.setdefault("cross", len(numbers))],
        recv_sem=recv_sem.at[numbers["cross"]], device_id=mate, device_id_type=MESH)
    cross.start()
    pending.append(cross)

    pltpu.make_async_remote_copy(
        src_ref=spare, dst_ref=src.at[y, pl.ds(x * 16 + (1 - k) * 8, PER)],
        send_sem=send_sem.at[numbers["cross"]], recv_sem=recv_sem.at[numbers["cross"]],
        device_id=mate, device_id_type=MESH).wait_recv()
    for q in (0, 1):
        first_out(q)
    for q in (0, 1):
        second_out(q, 0)
    for c in up:
        send(("m", 0, c), tgt_chunk(0, c, k), mate)

    waiting = [(turn, 0, c, k) for c in up] + [(take_mate, 0, c) for c in up]

    def work(n):
        for job in waiting[:n]:
            job[0](*job[1:])
        del waiting[:n]

    def targets_in(hop, c, e):
        for d, dz, at in ((1, -hop, c), (-1, hop, e)):
            if hop < 4 or at in (up[:chunks // 2] if d == 1 else up[chunks // 2:]):
                on = hop < 3 or (hop == 3 and at in (up[:chunks // 2] if d == 1 else up[chunks // 2:]))
                take_target(d, dz, at, (d,) if on else ())
                waiting.append((turn, dz, at, k))
                waiting.append((take_mate, dz, at))

    def sources_in(hop):
        for q in (0, 1):
            if hop == 1:
                for d in (1, -1):
                    first_in(q, d)
                    second_out(q, -d)
            elif hop == 2:
                second_in(q, 0)
                first_in(q, 2)
                second_out(q, 2)
            elif hop == 3:
                second_in(q, 1)
                second_in(q, -1)
            else:
                second_in(q, 2)

    for hop in range(1, 5):
        for i, (c, e) in enumerate(zip(up, down)):
            targets_in(hop, c, e)
            if i == EARLY:
                sources_in(hop)
            if hop == 1 and i == chunks - 1:
                edge_list(z, x, kept, counts, home, edges_ref, has_row_ref, has_col_ref)
                for at in range(YS):
                    src[at, SOURCES] = idle[...].astype(BF16)
            work(4)
    work(len(waiting))
    for q in (0, 1):
        for e in (0, -1, 1, 2):
            second_far(q, e)
    for copy in pending:
        copy.wait_send()


MESSAGES = 128


def collect(sp, tp, f, g, kept, counts, home):
    vmem = pl.BlockSpec(memory_space=pltpu.VMEM)
    shape = jax.ShapeDtypeStruct
    return pl.pallas_call(
        collect_kernel,
        out_shape=(
            shape((YS, SOURCES + 1, 32, 128), BF16),
            shape((TARGETS, 256, 48), BF16),
            shape((8, LIST), I32),
            shape((SOURCES, 128), F32),
            shape((TARGETS, 128), F32),
            shape((PER, 256), F32),
            shape((PER, 256), F32),
            shape((PER, 256), F32),
        ),
        in_specs=[vmem] * 8,
        out_specs=(vmem,) * 8,
        scratch_shapes=[
            pltpu.VMEM((PER, 32, 128), BF16),
            pltpu.VMEM((ZS, 2, PER, 32, 256), BF16),
            pltpu.SemaphoreType.DMA((MESSAGES,)),
            pltpu.SemaphoreType.DMA((MESSAGES,)),
        ],
        compiler_params=pltpu.CompilerParams(
            collective_id=0, has_side_effects=True, vmem_limit_bytes=32 * 2**20),
        name="collect",
    )(idle_source(), sp, tp, f, g, kept, counts, home)


def tiles_kernel(edge_vmem, src, turned, has_row_ref, has_col_ref, row_ref, col_ref,
                 edge_ref, row_acc, col_acc, edge_sem):
    load = pltpu.make_async_copy(edge_vmem, edge_ref, edge_sem)
    load.start()
    width = turned.shape[1]
    tail = jnp.where(iota((16, YS * 128), 0) >= 14, 1.0, 0.0).astype(BF16)
    row_acc[...] = jnp.zeros(row_acc.shape, F32)
    col_acc[...] = jnp.zeros(col_acc.shape, F32)
    load.wait()
    count = edge_ref[1, 0]

    def scores(s, p):
        cells = jnp.concatenate([src[at, s] for at in range(YS)], axis=1)
        right = jnp.concatenate([cells, tail], axis=0)
        return jnp.dot(turned[p], right, preferred_element_type=F32)

    def edge(at):
        code = edge_ref[0, at]
        s, p = code // TARGETS, code % TARGETS
        e = jnp.exp2(scores(s, p) * EXP2_SCALE)
        q = (e[:, 0:128] + e[:, 128:256]) + (e[:, 256:384] + e[:, 384:512])
        row_acc[s] += e.reshape(width // 8, 8, YS * 128).sum(axis=0)
        col_acc[p] += q.T.reshape(16, 8, width).sum(axis=0)

    def step(start, size):
        def run(it, _):
            for u in range(size):
                edge(start + it * size + u)
            return 0

        return run

    wide = (count + SLIM - 1) // WIDE
    lax.fori_loop(0, wide, step(0, WIDE), 0)
    rest = jnp.maximum(count - wide * WIDE, 0)
    lax.fori_loop(0, (rest + SLIM - 1) // SLIM, step(wide * WIDE, SLIM), 0)

    row_sum = jnp.sum(row_acc[0:SOURCES], axis=1)
    col_sum = jnp.sum(col_acc[...], axis=1)
    has_row = has_row_ref[:, 0:1] > 0.0
    has_col = has_col_ref[:, 0:1] > 0.0

    def outside(has, total):
        good = (total >= 2.0**-90) & (total <= 2.0**120)
        return jnp.max(jnp.where(has & jnp.logical_not(good), 1.0, 0.0))

    row_ref[...] = jnp.where(has_row, jnp.log(jnp.where(has_row, row_sum, 1.0)), LOW)
    col_ref[...] = jnp.where(has_col, jnp.log(jnp.where(has_col, col_sum, 1.0)), LOW)
    spread = jnp.maximum(outside(has_row, row_sum), outside(has_col, col_sum))

    @pl.when(spread > 0.0)
    def _():
        row_ref[...] = jnp.full(row_ref.shape, LOW, F32)
        col_ref[...] = jnp.full(col_ref.shape, LOW, F32)

        def merge(values, ref, at):
            top = jnp.max(values, axis=0, keepdims=True)
            here = top + jnp.log(jnp.sum(jnp.exp(values - top), axis=0, keepdims=True))
            old = ref[pl.ds(at, 1), :]
            peak = jnp.maximum(here, old)
            ref[pl.ds(at, 1), :] = peak + jnp.log(jnp.exp(here - peak) + jnp.exp(old - peak))

        def careful(e, _):
            code = edge_ref[0, e]
            s, p = code // TARGETS, code % TARGETS
            value = SHARP * scores(s, p)
            merge(value, row_ref, s)
            merge(value.T, col_ref, p)
            return 0

        lax.fori_loop(0, count, careful, 0)


def tiles(edges, src, turned, has_row, has_col):
    vmem = pl.BlockSpec(memory_space=pltpu.VMEM)
    shape = jax.ShapeDtypeStruct
    return pl.pallas_call(
        tiles_kernel,
        out_shape=(shape((SOURCES, YS * 128), F32), shape((TARGETS, 256), F32)),
        in_specs=[vmem] * 5,
        out_specs=(vmem, vmem),
        scratch_shapes=[
            pltpu.SMEM((8, LIST), I32),
            pltpu.VMEM((SOURCES + 1, 8, YS * 128), F32),
            pltpu.VMEM((TARGETS, 8, 256), F32),
            pltpu.SemaphoreType.DMA,
        ],
        compiler_params=pltpu.CompilerParams(vmem_limit_bytes=32 * 2**20),
        name="tiles",
    )(edges, src, turned, has_row, has_col)


def log_sum(parts):
    top = functools.reduce(jnp.maximum, parts)
    return top + jnp.log(sum(jnp.exp(part - top) for part in parts))


def settle_kernel(row, col, src_base, tgt_base, kept_pot, src_out, tgt_out,
                  row_y, row_x, col_z, wide, row_mid, send_sem, recv_sem):
    z, x, k, y = place()
    turn = lambda at, by, n: lax.rem(at + by, n)
    row_moves = [(dk, dy) for dk in (1, 0) for dy in (2, 1, 3, 0) if dk or dy]
    col_moves = [(dz, dk) for dz in (4, 3, 5, 2, 6, 1, 7, 0) for dk in (1, 0) if dz or dk]
    core = lambda dk: turn(k, dk, 2)
    xs = [device(z, turn(x, d, XS), k, y) for d in (2, 1, 3)]
    ys = [device(z, x, k, turn(y, d, YS)) for d in (2, 1, 3)]
    row_to = [device(z, x, core(dk), turn(y, dy, YS)) for dk, dy in row_moves]
    col_to = [device(turn(z, dz, ZS), x, core(dk), y) for dz, dk in col_moves]
    barrier = pltpu.get_barrier_semaphore()
    everyone = [to for to, (dz, dk) in zip(col_to, col_moves) if dz] + row_to + xs
    for other in everyone:
        pl.semaphore_signal(barrier, inc=1, device_id=other, device_id_type=MESH)
    pl.semaphore_wait(barrier, len(everyone))
    used = [0]

    def send(src_ref, dst_ref, to):
        m = used[0]
        used[0] += 1
        copy = pltpu.make_async_remote_copy(
            src_ref=src_ref, dst_ref=dst_ref, send_sem=send_sem.at[m], recv_sem=recv_sem.at[m],
            device_id=to, device_id_type=MESH)
        copy.start()
        return copy

    def quarter(at):
        return pl.ds(pl.multiple_of(at * 128, 128), 128)

    cols = [send(col.at[turn(z, dz, ZS), core(dk)], col_z.at[i], col_to[i]) for i, (dz, dk) in enumerate(col_moves)]
    rows = [send(row.at[:, core(dk), :, quarter(turn(y, dy, YS))], row_y.at[i], row_to[i])
            for i, (dk, dy) in enumerate(row_moves)]
    for copy in rows:
        copy.wait_recv()
    own = row[:, k, :, quarter(y)]
    row_mid[:, k] = log_sum([own] + [row_y[i] for i, (dk, _) in enumerate(row_moves) if dk == 0])
    row_mid[:, 1 - k] = log_sum([row_y[i] for i, (dk, _) in enumerate(row_moves) if dk == 1])

    across = [send(row_mid.at[turn(x, d, XS)], row_x.at[i], xs[i]) for i, d in enumerate((2, 1, 3))]
    for copy in cols:
        copy.wait_recv()
    total = log_sum([col[z, k]] + [col_z[i] for i in range(len(col_moves))])
    wide[y] = jnp.where(total > 0.5 * LOW, -0.25 * total + tgt_base[...], kept_pot[...])
    shares = [send(wide.at[y], wide.at[y], ys[i]) for i in range(YS - 1)]
    for copy in across:
        copy.wait_recv()
    ends = log_sum([row_mid[x]] + [row_x[i] for i in range(XS - 1)])
    src_out[:, 0:128] = src_base[:, 0:128] - 0.25 * ends[0]
    src_out[:, 128:256] = src_base[:, 128:256] - 0.25 * ends[1]
    for i, d in enumerate((2, 1, 3)):
        m = used[0] - (YS - 1) + i
        came = wide.at[turn(y, YS - d, YS)]
        pltpu.make_async_remote_copy(
            src_ref=came, dst_ref=came, send_sem=send_sem.at[m], recv_sem=recv_sem.at[m],
            device_id=ys[i], device_id_type=MESH).wait_recv()
    for at in range(YS):
        tgt_out[:, at * 256:(at + 1) * 256] = wide[at]
    for copy in cols + rows + across + shares:
        copy.wait_send()


def settle(row, col, src_base, tgt_base, kept_pot):
    vmem = pl.BlockSpec(memory_space=pltpu.VMEM)
    shape = jax.ShapeDtypeStruct
    return pl.pallas_call(
        settle_kernel,
        out_shape=(shape((PER, 256), F32), shape((PER, 1024), F32)),
        in_specs=[vmem] * 5,
        out_specs=(vmem, vmem),
        scratch_shapes=[
            pltpu.VMEM((7, XS, PER, 128), F32),
            pltpu.VMEM((XS - 1, 2, PER, 128), F32),
            pltpu.VMEM((15, PER, 256), F32),
            pltpu.VMEM((YS, PER, 256), F32),
            pltpu.VMEM((XS, 2, PER, 128), F32),
            pltpu.SemaphoreType.DMA((32,)),
            pltpu.SemaphoreType.DMA((32,)),
        ],
        compiler_params=pltpu.CompilerParams(
            collective_id=1, has_side_effects=True, vmem_limit_bytes=32 * 2**20),
        name="settle",
    )(row.reshape(XS, 2, PER, YS * 128), col.reshape(ZS, 2, PER, 256), src_base, tgt_base, kept_pot)


def local(sp, tp, f, g, kept, counts, home):
    src, turned, edges, has_row, has_col, src_base, tgt_base, kept_pot = collect(
        jnp.swapaxes(sp, 0, 1), jnp.swapaxes(tp, 0, 1), f, g, kept.T, counts.reshape(1, -1), home.reshape(1, -1))
    row, col = tiles(edges, src, turned, has_row, has_col)
    return settle(row, col, src_base, tgt_base, kept_pot)


def solution(mesh):
    placed = (
        P("clusters", None, "tiles"),
        P("clusters", None, None),
        P("clusters", "tiles"),
        P("clusters", None),
        P(),
        P(),
        P(),
    )
    return jax.shard_map(
        local,
        mesh=mesh,
        in_specs=placed,
        out_specs=(P("clusters", "tiles"), P("clusters", None)),
        check_vma=False,
    )
```

time: 139 us -> 129 us (0.928)
  the two profiles are of different devices: /device:TPU:6 before, /device:TPU:1 now
where the time goes in v2:
time: 129 us
  Pallas kernels  126 us (98%)
  local copies, waits for them, and re-layouts  2.33 us (2%)
    pallas_call x1, Pallas kernels, tiles(): pl.pallas_call(tiles_kernel, out_shape=(shape((SOURCES, YS * 128), F32),...  57.2 us
    pallas_call x1, Pallas kernels, settle(): pl.pallas_call(settle_kernel, out_shape=(shape((PER, 256), F32), shape((P...  40.4 us
    pallas_call x1, Pallas kernels, collect(): pl.pallas_call(collect_kernel, out_shape=(shape((YS, SOURCES + 1, 32, 128...  27.6 us

profile of v2, /device:TPU:1, one launch (start us, length us, event | category | flops | bytes accessed | tf_op | source)
XLA Modules:
  0.0 129.0 jit_solution(11108199415284670246)
XLA Ops:
  0.6 0.0 copy-start
  0.6 0.0 copy-start.1
  0.7 0.0 copy-start.2
  0.7 0.0 copy-start.3
  0.7 0.0 copy-start.5
  0.7 0.0 copy-start.6
  0.7 0.0 copy-start.7
  0.7 0.6 idle.1
  1.3 0.4 copy-done
  1.7 0.0 copy-done.1
  1.7 0.0 copy-done.2
  1.7 0.0 copy-done.3
  1.7 0.0 copy-done.5
  1.7 0.0 copy-done.6
  1.7 0.0 copy-done.7
  1.7 0.0 copy-start.4
  1.7 0.7 copy-done.4
  2.4 27.6 %collect.1 = (bf16[4,65,32,128]{3,2,1,0:T(8,128)(2,1)S(1)}, bf16[128,256,48]{2,1,0:T(8,128)(2,1)S(1)}, s32[8,256]{1,0:T(8,128)S(1)}, f32[64,128]{1,0:T(8,128)S(1...) custom-call(f32[32,128]{1,0:T(8,128)S(1)} %copy-done.4, ...), custom_call_target="tpu_custom_call" | custom-call | tf_op jit(solution)/shard_map/collect/pallas_call | solution.py:286
  30.1 57.2 %tiles.1 = (f32[64,512]{1,0:T(8,128)S(1)}, f32[128,256]{1,0:T(8,128)S(1)}) custom-call(s32[8,256]{1,0:T(8,128)S(1)} %get-tuple-element.12.edge_vmem, bf16[4,65,32,128]{3,2,1,0:T(8,128)(2,1)S(1)} %get-tuple-element.13.src, bf16[128,256,48]{2,1,0:T(8,128)(2,1)S(1)} %get-tuple-element.14.turned, f32[64,128]{1,0:T(8,128)S(1)} %get-tuple-element.15.has_row_ref, ...), custom_call_target="tpu_custom_call" | custom-call | tf_op jit(solution)/shard_map/tiles/pallas_call | solution.py:388
  87.3 40.4 %settle.1 = (f32[8,256]{1,0:T(8,128)S(1)}, f32[8,1024]{1,0:T(8,128)S(1)}) custom-call(f32[4,2,8,512]{3,2,1,0:T(8,128)S(1)} %bitcast.8, f32[8,2,8,256]{3,2,1,0:T(8,128)S(1)} %bitcast.9, f32[8,256]{1,0:T(8,128)S(1)} %get-tuple-element.19.src_base, f32[8,256]{1,0:T(8,128)S(1)} %get-tuple-element.20.tgt_base, f32[8,256]{1,0:T(8,128)S(1)} %get-tuple-element.21.kept_pot), custom_call_target="tpu_custom_call" | custom-call | tf_op jit(solution)/shard_map/settle/pallas_call | solution.py:474
  127.7 0.6 copy.11
  128.3 0.6 copy.12
Async XLA Ops:
  0.6 1.0 copy-start
  0.6 1.0 copy-start.1
  0.7 1.0 copy-start.2
  0.7 1.0 copy-start.3
  0.7 1.0 copy-start.5
  0.7 1.0 copy-start.6
  0.7 1.0 copy-start.7
  1.7 0.7 copy-start.4

commit v3 on v2

--- a/solution.py
+++ b/solution.py
@@ -45,7 +45,7 @@
     return high + low + half_norm
 
 
-def edge_list(z, x, kept, counts, home, edges_ref, has_row_ref, has_col_ref):
+def edge_list(z, x, kept, counts, home, edges_ref, has_row_ref, has_col_ref, no_row_ref, no_col_ref):
     lane = iota((SOURCES, 512), 1)
     row = iota((SOURCES, 512), 0)
     mine = lane == row + z * SOURCES
@@ -74,10 +74,12 @@
     number = jnp.sum(total, axis=0, keepdims=True)
     chosen = jnp.where(listed > 0.0, listed - 1.0, float(SOURCES * TARGETS)).astype(I32)
     edges_ref[...] = jnp.where(iota((8, LIST), 0) == 0, chosen, number.astype(I32))
-    has_row_ref[...] = jnp.broadcast_to(jnp.where(total > 0.0, 1.0, 0.0), has_row_ref.shape)
+    has_row = jnp.where(total > 0.0, 1.0, 0.0)
     named = (iota((TARGETS, LIST), 0) == (chosen & (TARGETS - 1))) & (listed > 0.0)
-    has_col_ref[...] = jnp.broadcast_to(
-        jnp.max(jnp.where(named, 1.0, 0.0), axis=1, keepdims=True), has_col_ref.shape)
+    has_col = jnp.max(jnp.where(named, 1.0, 0.0), axis=1, keepdims=True)
+    for has, has_ref, no_ref in ((has_row, has_row_ref, no_row_ref), (has_col, has_col_ref, no_col_ref)):
+        has_ref[...] = jnp.broadcast_to(has, has_ref.shape)
+        no_ref[...] = jnp.broadcast_to((1.0 - has_ref[...])[:, None, :], no_ref.shape)
 
 
 def idle_kernel(out):
@@ -90,12 +92,12 @@
         out_shape=jax.ShapeDtypeStruct((32, 128), F32),
         out_specs=pl.BlockSpec(memory_space=pltpu.VMEM),
         name="idle",
-        cost_estimate=pl.CostEstimate(flops=10**10, bytes_accessed=10**7, transcendentals=0),
+        cost_estimate=pl.CostEstimate(flops=10**10, bytes_accessed=3 * 10**7, transcendentals=0),
     )()
 
 
 def collect_kernel(idle, sp, tp, f, g, kept, counts, home,
-                   src, turned, edges_ref, has_row_ref, has_col_ref, src_base, tgt_base, kept_pot,
+                   src, turned, edges_ref, has_row_ref, has_col_ref, no_row_ref, no_col_ref, src_base, tgt_base, kept_pot,
                    spare, tgt, send_sem, recv_sem):
     z, x, k, y = place()
     step = lambda at, by, n: lax.rem(at + (by + n), n)
@@ -265,7 +267,7 @@
             if i == EARLY:
                 sources_in(hop)
             if hop == 1 and i == chunks - 1:
-                edge_list(z, x, kept, counts, home, edges_ref, has_row_ref, has_col_ref)
+                edge_list(z, x, kept, counts, home, edges_ref, has_row_ref, has_col_ref, no_row_ref, no_col_ref)
                 for at in range(YS):
                     src[at, SOURCES] = idle[...].astype(BF16)
             work(4)
@@ -291,12 +293,14 @@
             shape((8, LIST), I32),
             shape((SOURCES, 128), F32),
             shape((TARGETS, 128), F32),
+            shape((SOURCES, 8, 128), F32),
+            shape((TARGETS, 8, 128), F32),
             shape((PER, 256), F32),
             shape((PER, 256), F32),
             shape((PER, 256), F32),
         ),
         in_specs=[vmem] * 8,
-        out_specs=(vmem,) * 8,
+        out_specs=(vmem,) * 10,
         scratch_shapes=[
             pltpu.VMEM((PER, 32, 128), BF16),
             pltpu.VMEM((ZS, 2, PER, 32, 256), BF16),
@@ -309,14 +313,14 @@
     )(idle_source(), sp, tp, f, g, kept, counts, home)
 
 
-def tiles_kernel(edge_vmem, src, turned, has_row_ref, has_col_ref, row_ref, col_ref,
-                 edge_ref, row_acc, col_acc, edge_sem):
+def tiles_kernel(edge_vmem, src, turned, no_row, no_col, row_acc, col_acc, wild_ref, edge_ref, edge_sem):
     load = pltpu.make_async_copy(edge_vmem, edge_ref, edge_sem)
     load.start()
     width = turned.shape[1]
     tail = jnp.where(iota((16, YS * 128), 0) >= 14, 1.0, 0.0).astype(BF16)
-    row_acc[...] = jnp.zeros(row_acc.shape, F32)
-    col_acc[...] = jnp.zeros(col_acc.shape, F32)
+    row_acc[0:SOURCES] = jnp.concatenate([no_row[...]] * YS, axis=2)
+    row_acc[SOURCES] = jnp.zeros((8, YS * 128), F32)
+    col_acc[...] = jnp.concatenate([no_col[...]] * 2, axis=2)
     load.wait()
     count = edge_ref[1, 0]
 
@@ -346,59 +350,53 @@
     rest = jnp.maximum(count - wide * WIDE, 0)
     lax.fori_loop(0, (rest + SLIM - 1) // SLIM, step(wide * WIDE, SLIM), 0)
 
-    row_sum = jnp.sum(row_acc[0:SOURCES], axis=1)
-    col_sum = jnp.sum(col_acc[...], axis=1)
-    has_row = has_row_ref[:, 0:1] > 0.0
-    has_col = has_col_ref[:, 0:1] > 0.0
-
-    def outside(has, total):
-        good = (total >= 2.0**-90) & (total <= 2.0**120)
-        return jnp.max(jnp.where(has & jnp.logical_not(good), 1.0, 0.0))
-
-    row_ref[...] = jnp.where(has_row, jnp.log(jnp.where(has_row, row_sum, 1.0)), LOW)
-    col_ref[...] = jnp.where(has_col, jnp.log(jnp.where(has_col, col_sum, 1.0)), LOW)
-    spread = jnp.maximum(outside(has_row, row_sum), outside(has_col, col_sum))
-
-    @pl.when(spread > 0.0)
+    low = jnp.minimum(jnp.min(row_acc[0:SOURCES]), jnp.min(col_acc[...]))
+    high = jnp.maximum(jnp.max(row_acc[0:SOURCES]), jnp.max(col_acc[...]))
+    wild = jnp.logical_not((low >= 2.0**-90) & (high <= 2.0**116))
+    wild_ref[...] = jnp.where(wild, jnp.ones(wild_ref.shape, F32), 0.0)
+
+    @pl.when(wild)
     def _():
-        row_ref[...] = jnp.full(row_ref.shape, LOW, F32)
-        col_ref[...] = jnp.full(col_ref.shape, LOW, F32)
+        row_acc[...] = jnp.full(row_acc.shape, LOW, F32)
+        col_acc[...] = jnp.full(col_acc.shape, LOW, F32)
 
         def merge(values, ref, at):
             top = jnp.max(values, axis=0, keepdims=True)
             here = top + jnp.log(jnp.sum(jnp.exp(values - top), axis=0, keepdims=True))
-            old = ref[pl.ds(at, 1), :]
+            old = ref[at, 0:1, :]
             peak = jnp.maximum(here, old)
-            ref[pl.ds(at, 1), :] = peak + jnp.log(jnp.exp(here - peak) + jnp.exp(old - peak))
+            ref[at, 0:1, :] = peak + jnp.log(jnp.exp(here - peak) + jnp.exp(old - peak))
 
         def careful(e, _):
             code = edge_ref[0, e]
             s, p = code // TARGETS, code % TARGETS
             value = SHARP * scores(s, p)
-            merge(value, row_ref, s)
-            merge(value.T, col_ref, p)
+            merge(value, row_acc, s)
+            merge(value.T, col_acc, p)
             return 0
 
         lax.fori_loop(0, count, careful, 0)
 
 
-def tiles(edges, src, turned, has_row, has_col):
+def tiles(edges, src, turned, no_row, no_col):
     vmem = pl.BlockSpec(memory_space=pltpu.VMEM)
     shape = jax.ShapeDtypeStruct
     return pl.pallas_call(
         tiles_kernel,
-        out_shape=(shape((SOURCES, YS * 128), F32), shape((TARGETS, 256), F32)),
+        out_shape=(
+            shape((SOURCES + 1, 8, YS * 128), F32),
+            shape((TARGETS, 8, 256), F32),
+            shape((8, 128), F32),
+        ),
         in_specs=[vmem] * 5,
-        out_specs=(vmem, vmem),
+        out_specs=(vmem,) * 3,
         scratch_shapes=[
             pltpu.SMEM((8, LIST), I32),
-            pltpu.VMEM((SOURCES + 1, 8, YS * 128), F32),
-            pltpu.VMEM((TARGETS, 8, 256), F32),
             pltpu.SemaphoreType.DMA,
         ],
         compiler_params=pltpu.CompilerParams(vmem_limit_bytes=32 * 2**20),
         name="tiles",
-    )(edges, src, turned, has_row, has_col)
+    )(edges, src, turned, no_row, no_col)
 
 
 def log_sum(parts):
@@ -406,8 +404,8 @@
     return top + jnp.log(sum(jnp.exp(part - top) for part in parts))
 
 
-def settle_kernel(row, col, src_base, tgt_base, kept_pot, src_out, tgt_out,
-                  row_y, row_x, col_z, wide, row_mid, send_sem, recv_sem):
+def settle_kernel(row_acc, col_acc, wild_ref, has_row, has_col, src_base, tgt_base, kept_pot, src_out, tgt_out,
+                  row, col, row_y, row_x, col_z, wide, row_mid, send_sem, recv_sem):
     z, x, k, y = place()
     turn = lambda at, by, n: lax.rem(at + by, n)
     row_moves = [(dk, dy) for dk in (1, 0) for dy in (2, 1, 3, 0) if dk or dy]
@@ -421,6 +419,16 @@
     everyone = [to for to, (dz, dk) in zip(col_to, col_moves) if dz] + row_to + xs
     for other in everyone:
         pl.semaphore_signal(barrier, inc=1, device_id=other, device_id_type=MESH)
+
+    wild = wild_ref[0:1, 0:1] > 0.0
+
+    def logs(acc, has, out):
+        has = has[:, 0:1] > 0.0
+        total = jnp.where(has, jnp.sum(acc, axis=1), 1.0)
+        out[...] = jnp.where(has, jnp.where(wild, acc[:, 0], jnp.log(total)), LOW).reshape(out.shape)
+
+    logs(row_acc[0:SOURCES], has_row, row)
+    logs(col_acc[...], has_col, col)
     pl.semaphore_wait(barrier, len(everyone))
     used = [0]
 
@@ -468,15 +476,17 @@
         copy.wait_send()
 
 
-def settle(row, col, src_base, tgt_base, kept_pot):
+def settle(row_acc, col_acc, wild, has_row, has_col, src_base, tgt_base, kept_pot):
     vmem = pl.BlockSpec(memory_space=pltpu.VMEM)
     shape = jax.ShapeDtypeStruct
     return pl.pallas_call(
         settle_kernel,
         out_shape=(shape((PER, 256), F32), shape((PER, 1024), F32)),
-        in_specs=[vmem] * 5,
+        in_specs=[vmem] * 8,
         out_specs=(vmem, vmem),
         scratch_shapes=[
+            pltpu.VMEM((XS, 2, PER, YS * 128), F32),
+            pltpu.VMEM((ZS, 2, PER, 256), F32),
             pltpu.VMEM((7, XS, PER, 128), F32),
             pltpu.VMEM((XS - 1, 2, PER, 128), F32),
             pltpu.VMEM((15, PER, 256), F32),
@@ -488,14 +498,14 @@
         compiler_params=pltpu.CompilerParams(
             collective_id=1, has_side_effects=True, vmem_limit_bytes=32 * 2**20),
         name="settle",
-    )(row.reshape(XS, 2, PER, YS * 128), col.reshape(ZS, 2, PER, 256), src_base, tgt_base, kept_pot)
+    )(row_acc, col_acc, wild, has_row, has_col, src_base, tgt_base, kept_pot)
 
 
 def local(sp, tp, f, g, kept, counts, home):
-    src, turned, edges, has_row, has_col, src_base, tgt_base, kept_pot = collect(
+    src, turned, edges, has_row, has_col, no_row, no_col, src_base, tgt_base, kept_pot = collect(
         jnp.swapaxes(sp, 0, 1), jnp.swapaxes(tp, 0, 1), f, g, kept.T, counts.reshape(1, -1), home.reshape(1, -1))
-    row, col = tiles(edges, src, turned, has_row, has_col)
-    return settle(row, col, src_base, tgt_base, kept_pot)
+    row_acc, col_acc, wild = tiles(edges, src, turned, no_row, no_col)
+    return settle(row_acc, col_acc, wild, has_row, has_col, src_base, tgt_base, kept_pot)
 
 
 def solution(mesh):

time: 129 us -> 138 us (1.070)
  the two profiles are of different devices: /device:TPU:1 before, /device:TPU:6 now
where the time goes in v3:
time: 138 us; the launch traced here: 137 us
  Pallas kernels  134 us (97%)
  local copies, waits for them, and re-layouts  2.33 us (2%)
    pallas_call x1, Pallas kernels, tiles(): pl.pallas_call(tiles_kernel, out_shape=(shape((SOURCES + 1, 8, YS * 128),...  79.1 us
    pallas_call x1, Pallas kernels, settle(): pl.pallas_call(settle_kernel, out_shape=(shape((PER, 256), F32), shape((P...  28.3 us
    pallas_call x1, Pallas kernels, collect(): pl.pallas_call(collect_kernel, out_shape=(shape((YS, SOURCES + 1, 32, 128...  26.4 us

profile of v3, /device:TPU:6, one launch (start us, length us, event | category | flops | bytes accessed | tf_op | source)
XLA Modules:
  0.0 137.4 jit_solution(11438394249634811542)
XLA Ops:
  0.6 0.0 copy-start
  0.6 0.0 copy-start.1
  0.7 0.0 copy-start.2
  0.7 0.0 copy-start.3
  0.7 0.0 copy-start.5
  0.7 0.0 copy-start.6
  0.7 0.0 copy-start.7
  0.7 0.6 idle.1
  1.3 0.4 copy-done
  1.7 0.0 copy-done.1
  1.7 0.0 copy-done.2
  1.7 0.0 copy-done.3
  1.7 0.0 copy-done.5
  1.7 0.0 copy-done.6
  1.7 0.0 copy-done.7
  1.7 0.0 copy-start.4
  1.7 0.7 copy-done.4
  2.4 26.4 %collect.1 = (bf16[4,65,32,128]{3,2,1,0:T(8,128)(2,1)S(1)}, bf16[128,256,48]{2,1,0:T(8,128)(2,1)S(1)}, s32[8,256]{1,0:T(8,128)S(1)}, f32[64,128]{1,0:T(8,128)S(1...) custom-call(f32[32,128]{1,0:T(8,128)S(1)} %copy-done.4, ...), custom_call_target="tpu_custom_call" | custom-call | tf_op jit(solution)/shard_map/collect/pallas_call | solution.py:288
  28.8 79.1 %tiles.1 = (f32[65,8,512]{2,1,0:T(8,128)S(1)}, f32[128,8,256]{2,1,0:T(8,128)S(1)}, f32[8,128]{1,0:T(8,128)S(1)}) custom-call(s32[8,256]{1,0:T(8,128)S(1)} %get-tuple-element.15.edge_vmem, bf16[4,65,32,128]{3,2,1,0:T(8,128)(2,1)S(1)} %get-tuple-element.16.src, bf16[128,256,48]{2,1,0:T(8,128)(2,1)S(1)} %get-tuple-element.17.turned, ...), custom_call_target="tpu_custom_call" | custom-call | tf_op jit(solution)/shard_map/tiles/pallas_call | solution.py:384
  107.9 28.3 %settle.1 = (f32[8,256]{1,0:T(8,128)S(1)}, f32[8,1024]{1,0:T(8,128)S(1)}) custom-call(f32[65,8,512]{2,1,0:T(8,128)S(1)} %get-tuple-element.20.row_acc, f32[128,8,256]{2,1,0:T(8,128)S(1)} %get-tuple-element.21.col_acc, f32[8,128]{1,0:T(8,128)S(1)} %get-tuple-element.22.wild_ref, f32[64,128]{1,0:T(8,128)S(1)} %get-tuple-element.23.has_row, ...), custom_call_target="tpu_custom_call" | custom-call | tf_op jit(solution)/shard_map/settle/pallas_call | solution.py:482
  136.2 0.6 copy.11
  136.8 0.6 copy.12
Async XLA Ops:
  0.6 1.0 copy-start
  0.6 1.0 copy-start.1
  0.7 1.0 copy-start.2
  0.7 1.0 copy-start.3
  0.7 1.0 copy-start.5
  0.7 1.0 copy-start.6
  0.7 1.0 copy-start.7
  1.7 0.7 copy-start.4

commit v4 on v3

--- a/solution.py
+++ b/solution.py
@@ -16,7 +16,7 @@
 SOURCES, TARGETS = XS * 2 * PER, ZS * 2 * PER
 LIST = 256
 CHUNK = 2
-EARLY = 1
+EARLY = 0
 WIDE, SLIM = 32, 8
 F32, BF16, I32 = jnp.float32, jnp.bfloat16, jnp.int32
 
@@ -83,13 +83,13 @@
 
 
 def idle_kernel(out):
-    out[...] = jnp.where(iota(out.shape, 0) == 30, LOW, 0.0)
-
-
-def idle_source():
+    out[...] = jnp.zeros(out.shape, F32)
+
+
+def idle_block():
     return pl.pallas_call(
         idle_kernel,
-        out_shape=jax.ShapeDtypeStruct((32, 128), F32),
+        out_shape=jax.ShapeDtypeStruct((8, 128), F32),
         out_specs=pl.BlockSpec(memory_space=pltpu.VMEM),
         name="idle",
         cost_estimate=pl.CostEstimate(flops=10**10, bytes_accessed=3 * 10**7, transcendentals=0),
@@ -269,7 +269,7 @@
             if hop == 1 and i == chunks - 1:
                 edge_list(z, x, kept, counts, home, edges_ref, has_row_ref, has_col_ref, no_row_ref, no_col_ref)
                 for at in range(YS):
-                    src[at, SOURCES] = idle[...].astype(BF16)
+                    src[at, SOURCES] = jnp.where(iota((32, 128), 0) == 30, LOW, 0.0).astype(BF16)
             work(4)
     work(len(waiting))
     for q in (0, 1):
@@ -299,7 +299,7 @@
             shape((PER, 256), F32),
             shape((PER, 256), F32),
         ),
-        in_specs=[vmem] * 8,
+        in_specs=[pl.BlockSpec(memory_space=pl.ANY)] + [vmem] * 7,
         out_specs=(vmem,) * 10,
         scratch_shapes=[
             pltpu.VMEM((PER, 32, 128), BF16),
@@ -310,7 +310,7 @@
         compiler_params=pltpu.CompilerParams(
             collective_id=0, has_side_effects=True, vmem_limit_bytes=32 * 2**20),
         name="collect",
-    )(idle_source(), sp, tp, f, g, kept, counts, home)
+    )(idle_block(), sp, tp, f, g, kept, counts, home)
 
 
 def tiles_kernel(edge_vmem, src, turned, no_row, no_col, row_acc, col_acc, wild_ref, edge_ref, edge_sem):

time: 138 us -> 129 us (0.935); the launches traced: 137 us -> 127 us
  Pallas kernels: 134 us -> 124 us
    pallas_call x1, Pallas kernels: 79.1 us -> 70 us  [tiles(): pl.pallas_call(tiles_kernel, out_shape=(shape((SOURCES + 1, 8, YS * 128),...]
where the time goes in v4:
time: 129 us; the launch traced here: 127 us
  Pallas kernels  124 us (96%)
  local copies, waits for them, and re-layouts  2.31 us (2%)
    pallas_call x1, Pallas kernels, tiles(): pl.pallas_call(tiles_kernel, out_shape=(shape((SOURCES + 1, 8, YS * 128),...  70 us
    pallas_call x1, Pallas kernels, settle(): pl.pallas_call(settle_kernel, out_shape=(shape((PER, 256), F32), shape((P...  27.2 us
    pallas_call x1, Pallas kernels, collect(): pl.pallas_call(collect_kernel, out_shape=(shape((YS, SOURCES + 1, 32, 128...  25.9 us

profile of v4, /device:TPU:6, one launch (start us, length us, event | category | flops | bytes accessed | tf_op | source)
XLA Modules:
  0.0 126.8 jit_solution(12337954435203239428)
XLA Ops:
  0.6 0.0 copy-start
  0.6 0.0 copy-start.1
  0.7 0.0 copy-start.2
  0.7 0.0 copy-start.3
  0.7 0.0 copy-start.4
  0.7 0.0 copy-start.6
  0.7 0.0 copy-start.7
  0.7 0.6 idle.1
  1.3 0.4 copy-done
  1.7 0.0 copy-done.1
  1.7 0.0 copy-done.2
  1.7 0.0 copy-done.3
  1.7 0.0 copy-done.4
  1.7 0.0 copy-done.6
  1.7 0.0 copy-done.7
  1.7 0.0 copy-start.5
  1.7 0.7 copy-done.5
  2.4 25.9 %collect.1 = (bf16[4,65,32,128]{3,2,1,0:T(8,128)(2,1)S(1)}, bf16[128,256,48]{2,1,0:T(8,128)(2,1)S(1)}, s32[8,256]{1,0:T(8,128)S(1)}, f32[64,128]{1,0:T(8,128)S(1...) custom-call(f32[8,128]{1,0:T(8,128)S(1)} %copy-done.5, ...), custom_call_target="tpu_custom_call" | custom-call | tf_op jit(solution)/shard_map/collect/pallas_call | solution.py:288
  28.3 70.0 %tiles.1 = (f32[65,8,512]{2,1,0:T(8,128)S(1)}, f32[128,8,256]{2,1,0:T(8,128)S(1)}, f32[8,128]{1,0:T(8,128)S(1)}) custom-call(s32[8,256]{1,0:T(8,128)S(1)} %get-tuple-element.15.edge_vmem, bf16[4,65,32,128]{3,2,1,0:T(8,128)(2,1)S(1)} %get-tuple-element.16.src, bf16[128,256,48]{2,1,0:T(8,128)(2,1)S(1)} %get-tuple-element.17.turned, ...), custom_call_target="tpu_custom_call" | custom-call | tf_op jit(solution)/shard_map/tiles/pallas_call | solution.py:384
  98.4 27.2 %settle.1 = (f32[8,256]{1,0:T(8,128)S(1)}, f32[8,1024]{1,0:T(8,128)S(1)}) custom-call(f32[65,8,512]{2,1,0:T(8,128)S(1)} %get-tuple-element.20.row_acc, f32[128,8,256]{2,1,0:T(8,128)S(1)} %get-tuple-element.21.col_acc, f32[8,128]{1,0:T(8,128)S(1)} %get-tuple-element.22.wild_ref, f32[64,128]{1,0:T(8,128)S(1)} %get-tuple-element.23.has_row, ...), custom_call_target="tpu_custom_call" | custom-call | tf_op jit(solution)/shard_map/settle/pallas_call | solution.py:482
  125.6 0.6 copy.11
  126.2 0.6 copy.12
Async XLA Ops:
  0.6 1.0 copy-start
  0.6 1.0 copy-start.1
  0.7 1.0 copy-start.2
  0.7 1.0 copy-start.3
  0.7 1.0 copy-start.4
  0.7 1.0 copy-start.6
  0.7 1.0 copy-start.7
  1.7 0.7 copy-start.5

commit v5 on v4

--- a/solution.py
+++ b/solution.py
@@ -270,7 +270,7 @@
                 edge_list(z, x, kept, counts, home, edges_ref, has_row_ref, has_col_ref, no_row_ref, no_col_ref)
                 for at in range(YS):
                     src[at, SOURCES] = jnp.where(iota((32, 128), 0) == 30, LOW, 0.0).astype(BF16)
-            work(4)
+            work(5 if hop == 3 else 4)
     work(len(waiting))
     for q in (0, 1):
         for e in (0, -1, 1, 2):

time: 129 us -> 126 us (0.977); the launches traced: 127 us -> 126 us
    pallas_call x1, Pallas kernels: 27.2 us -> 22.7 us  [settle(): pl.pallas_call(settle_kernel, out_shape=(shape((PER, 256), F32), shape((P...]
    pallas_call x1, Pallas kernels: 70 us -> 73.5 us  [tiles(): pl.pallas_call(tiles_kernel, out_shape=(shape((SOURCES + 1, 8, YS * 128),...]
where the time goes in v5:
time: 126 us
  Pallas kernels  123 us (98%)
  local copies, waits for them, and re-layouts  2.31 us (2%)
    pallas_call x1, Pallas kernels, tiles(): pl.pallas_call(tiles_kernel, out_shape=(shape((SOURCES + 1, 8, YS * 128),...  73.5 us
    pallas_call x1, Pallas kernels, collect(): pl.pallas_call(collect_kernel, out_shape=(shape((YS, SOURCES + 1, 32, 128...  25.9 us
    pallas_call x1, Pallas kernels, settle(): pl.pallas_call(settle_kernel, out_shape=(shape((PER, 256), F32), shape((P...  22.7 us

profile of v5, /device:TPU:6, one launch (start us, length us, event | category | flops | bytes accessed | tf_op | source)
XLA Modules:
  0.0 125.8 jit_solution(7252395109666667356)
XLA Ops:
  0.6 0.0 copy-start
  0.6 0.0 copy-start.1
  0.7 0.0 copy-start.2
  0.7 0.0 copy-start.3
  0.7 0.0 copy-start.4
  0.7 0.0 copy-start.6
  0.7 0.0 copy-start.7
  0.7 0.6 idle.1
  1.3 0.4 copy-done
  1.7 0.0 copy-done.1
  1.7 0.0 copy-done.2
  1.7 0.0 copy-done.3
  1.7 0.0 copy-done.4
  1.7 0.0 copy-done.6
  1.7 0.0 copy-done.7
  1.7 0.0 copy-start.5
  1.7 0.7 copy-done.5
  2.4 25.9 %collect.1 = (bf16[4,65,32,128]{3,2,1,0:T(8,128)(2,1)S(1)}, bf16[128,256,48]{2,1,0:T(8,128)(2,1)S(1)}, s32[8,256]{1,0:T(8,128)S(1)}, f32[64,128]{1,0:T(8,128)S(1...) custom-call(f32[8,128]{1,0:T(8,128)S(1)} %copy-done.5, ...), custom_call_target="tpu_custom_call" | custom-call | tf_op jit(solution)/shard_map/collect/pallas_call | solution.py:288
  28.3 73.5 %tiles.1 = (f32[65,8,512]{2,1,0:T(8,128)S(1)}, f32[128,8,256]{2,1,0:T(8,128)S(1)}, f32[8,128]{1,0:T(8,128)S(1)}) custom-call(s32[8,256]{1,0:T(8,128)S(1)} %get-tuple-element.15.edge_vmem, bf16[4,65,32,128]{3,2,1,0:T(8,128)(2,1)S(1)} %get-tuple-element.16.src, bf16[128,256,48]{2,1,0:T(8,128)(2,1)S(1)} %get-tuple-element.17.turned, ...), custom_call_target="tpu_custom_call" | custom-call | tf_op jit(solution)/shard_map/tiles/pallas_call | solution.py:384
  101.9 22.7 %settle.1 = (f32[8,256]{1,0:T(8,128)S(1)}, f32[8,1024]{1,0:T(8,128)S(1)}) custom-call(f32[65,8,512]{2,1,0:T(8,128)S(1)} %get-tuple-element.20.row_acc, f32[128,8,256]{2,1,0:T(8,128)S(1)} %get-tuple-element.21.col_acc, f32[8,128]{1,0:T(8,128)S(1)} %get-tuple-element.22.wild_ref, f32[64,128]{1,0:T(8,128)S(1)} %get-tuple-element.23.has_row, ...), custom_call_target="tpu_custom_call" | custom-call | tf_op jit(solution)/shard_map/settle/pallas_call | solution.py:482
  124.6 0.6 copy.11
  125.2 0.6 copy.12
Async XLA Ops:
  0.6 1.0 copy-start
  0.6 1.0 copy-start.1
  0.7 1.0 copy-start.2
  0.7 1.0 copy-start.3
  0.7 1.0 copy-start.4
  0.7 1.0 copy-start.6
  0.7 1.0 copy-start.7
  1.7 0.7 copy-start.5
